TPU v7x, 256 devices: a whole 4x4x8 slice. The times are simulated.
256 devices in a mesh: replica: 4 (over z_hi), fsdp: 16 (over y, z_lo, core), tensor: 4 (over x).
Axes of the slice: x: 4, y: 4, z: 8 (z_hi: 4, z_lo: 2; z = z_hi * 2 + z_lo), core: 2. Of those that a mesh axis runs over, the one named last changes fastest.
Arguments:
- inputs: bfloat16 [4, 8192, 8192], P('replica', 'fsdp'), may hold values from -6 to 6
- key_grad: bfloat16 [4, 8192, 1024], P('replica', 'fsdp', 'tensor'), may hold values from -0.75 to 0.75
- value_grad: bfloat16 [4, 8192, 1024], P('replica', 'fsdp', 'tensor'), may hold values from -0.75 to 0.75
- key_weight: bfloat16 [4, 8192, 1024], P('replica', 'fsdp', 'tensor'), may hold values from -0.0625 to 0.0625
- value_weight: bfloat16 [4, 8192, 1024], P('replica', 'fsdp', 'tensor'), may hold values from -0.0625 to 0.0625
- global_params: float32 [1024, 8192], P('fsdp', 'tensor'), may hold values from -6 to 6
- momentum: float32 [1024, 8192], P('fsdp', 'tensor'), may hold values from -6 to 6
- local_params: float32 [4, 1024, 8192], P('replica', 'fsdp', 'tensor'), may hold values from -6 to 6
- fragment: int32 [1], replicated, may hold values from 0 to 7
- step: int32 [1], replicated, may hold values from 0 to 127
- outer_rates: float32 [8], replicated, may hold values from 0.3 to 1
Outputs:
- input_grad: bfloat16 [4, 8192, 8192], P('replica', 'fsdp', 'tensor')
- key_wgrad: float32 [4, 8192, 1024], P('replica', 'fsdp', 'tensor')
- value_wgrad: float32 [4, 8192, 1024], P('replica', 'fsdp', 'tensor')
- new_global: float32 [1024, 8192], P('fsdp', 'tensor')
- new_momentum: float32 [1024, 8192], P('fsdp', 'tensor')
- new_local: float32 [4, 1024, 8192], P('replica', 'fsdp', 'tensor')
All inputs are finite; a program needn't handle non-finite values.
Results may differ from a plain program's by a relative error of at most 0.0095.
Values may be sent and summed in bfloat16 or wider, within the bound.
No kernel may reach another device: no remote copies, remote signals or barrier semaphores. Data moves between devices by JAX's collectives and lax.ppermute only.
A program may use at most 128 MiB of HBM per device.

v0:
```python
import jax
import jax.numpy as jnp
from jax import lax
from jax.sharding import PartitionSpec as P

WARMUP = 64


momentum_decay = 0.9
mixing = 0.5


def outer_step(global_part, momentum_part, average, rate):
    delta = global_part - average
    fresh_momentum = momentum_decay * momentum_part + delta
    fresh_global = global_part - rate * (delta + momentum_decay * fresh_momentum)
    return (fresh_global, fresh_momentum)


def local(
    inputs,
    key_grad,
    value_grad,
    key_weight,
    value_weight,
    global_params,
    momentum,
    local_params,
    fragment,
    step,
    outer_rates,
):
    tokens_in = inputs[0]
    grad_k = key_grad[0]
    grad_v = value_grad[0]
    term = lax.dot_general(
        grad_k,
        lax.all_gather(key_weight[0], "fsdp", axis=0, tiled=True),
        (((1,), (1,)), ((), ())),
        preferred_element_type=jnp.float32,
    )
    term = term + lax.dot_general(
        grad_v,
        lax.all_gather(value_weight[0], "fsdp", axis=0, tiled=True),
        (((1,), (1,)), ((), ())),
        preferred_element_type=jnp.float32,
    )
    back = lax.psum_scatter(term, "tensor", scatter_dimension=1, tiled=True).astype(jnp.bfloat16)
    heads_width = grad_k.shape[1]
    both_grad = jnp.concatenate([grad_k, grad_v], axis=1)
    summed = lax.psum_scatter(
        lax.dot_general(
            tokens_in, both_grad, (((0,), (0,)), ((), ())), preferred_element_type=jnp.float32
        ),
        "fsdp",
        scatter_dimension=0,
        tiled=True,
    )
    wgrad_k = summed[:, :heads_width]
    wgrad_v = summed[:, heads_width:]
    count_frag = outer_rates.shape[0]
    chosen = (jnp.arange(count_frag, dtype=jnp.int32) == fragment[0]).astype(jnp.float32)
    warm = jnp.minimum(1.0, (step[0].astype(jnp.float32) + 1.0) / WARMUP)
    rate = jnp.sum(chosen * outer_rates) * warm
    replicas = lax.axis_size("replica")
    local_now = local_params[0]
    total = lax.psum(local_now.astype(jnp.bfloat16), "replica").astype(jnp.float32)
    fresh_global, fresh_momentum = outer_step(global_params, momentum, total / replicas, rate)
    fresh_local = mixing * local_now + (1.0 - mixing) * fresh_global
    return (
        back[None],
        wgrad_k[None],
        wgrad_v[None],
        fresh_global,
        fresh_momentum,
        fresh_local[None],
    )


def solution(mesh):
    in_specs = (
        P("replica", "fsdp", None),
        P("replica", "fsdp", "tensor"),
        P("replica", "fsdp", "tensor"),
        P("replica", "fsdp", "tensor"),
        P("replica", "fsdp", "tensor"),
        P("fsdp", "tensor"),
        P("fsdp", "tensor"),
        P("replica", "fsdp", "tensor"),
        P(),
        P(),
        P(),
    )
    out_specs = (
        P("replica", "fsdp", "tensor"),
        P("replica", "fsdp", "tensor"),
        P("replica", "fsdp", "tensor"),
        P("fsdp", "tensor"),
        P("fsdp", "tensor"),
        P("replica", "fsdp", "tensor"),
    )
    return jax.shard_map(local, mesh=mesh, in_specs=in_specs, out_specs=out_specs, check_vma=False)
```

profile of v0, /device:TPU:6, one launch (start us, length us, event | category | flops | bytes accessed | tf_op | source)
XLA Modules:
  0.0 445.4 jit_solution(5449957928117956908)
XLA Ops:
  8.0 0.0 all-gather.5.cloned.1.call-start
  8.0 0.7 all-gather.5.cloned.1.call-update
  8.7 0.0 all-gather.7.cloned.1.call-start
  8.8 0.7 all-gather.7.cloned.1.call-update
  9.5 0.0 all-reduce.2.cloned.1.call-start
  9.5 1.8 bitcast_convert_fusion
  11.3 0.0 all-reduce.2.cloned.1.call-update
  11.3 0.0 reduce-scatter.5.cloned.1.call-start
  11.4 13.9 %convolution_bitcast_fusion = f32[8192,512]{0,1:T(8,128)} fusion(bf16[1,512,8192]{2,1,0:T(8,128)(2,1)} %param.11, bf16[512,256]{1,0:T(8,128)(2,1)} %bitcast.35, bf16[512,256]{1,0:T(8,128)(2,1)} %bitcast.36), kind=kOutput, calls=%fused_computation.1 | convolution fusion | flops 4296015872 | bytes 25690112 | tf_op jit(solution)/shard_map/dot_general | solution.py:52
  25.3 0.0 reduce-scatter.3.cloned.1.call-start
  25.4 30.1 %all-gather.5.cloned.1.call-done = bf16[1,8192,256]{2,1,0:T(8,128)(2,1)} async-done(((bf16[1,512,256]{2,1,0:T(8,128)(2,1)}), bf16[1,8192,256]{2,1,0:T(8,128)(2,1)}) %all-gather.5.cloned.1.call-update) | async-done | bytes 4194320 | tf_op jit(solution)/shard_map/all_gather | solution.py:38
  55.5 10.3 %fusion.2 = f32[512,8192]{1,0:T(8,128)} fusion(bf16[1,8192,256]{2,1,0:T(8,128)(2,1)} %all-gather.5.cloned.1.call-done, bf16[1,512,256]{2,1,0:T(8,128)(2,1)S(1)} %copy-done.2), kind=kOutput, calls=%fused_computation.4 | convolution fusion | flops 2147483648 | bytes 21233664 | tf_op jit(solution)/shard_map/dot_general | solution.py:36
  65.8 31.6 %all-gather.7.cloned.1.call-done = bf16[1,8192,256]{2,1,0:T(8,128)(2,1)} async-done(((bf16[1,512,256]{2,1,0:T(8,128)(2,1)}), bf16[1,8192,256]{2,1,0:T(8,128)(2,1)}) %all-gather.7.cloned.1.call-update) | async-done | bytes 4194320 | tf_op jit(solution)/shard_map/all_gather | solution.py:44
  97.3 15.8 %convolution_add_fusion = f32[512,8192]{1,0:T(8,128)} fusion(f32[512,8192]{1,0:T(8,128)} %fusion.2, bf16[1,8192,256]{2,1,0:T(8,128)(2,1)} %all-gather.7.cloned.1.call-done, bf16[1,512,256]{2,1,0:T(8,128)(2,1)S(1)} %copy-done.1), kind=kOutput, calls=%fused_computation | convolution fusion | flops 2151677952 | bytes 38010880 | tf_op jit(solution)/shard_map/dot_general | solution.py:42
  113.1 0.0 reduce-scatter.3.cloned.1.call-update
  114.6 0.6 fusion.9
  115.8 0.0 all-reduce.2.cloned.1.call-done
  115.9 2.2 fusion.8
  118.1 166.7 %reduce-scatter.5.cloned.1.call-done = f32[512,512]{0,1:T(8,128)} async-done(((f32[8192,512]{0,1:T(8,128)}), f32[512,512]{0,1:T(8,128)}) %reduce-scatter.5.cloned.1.call-update) | async-done | bytes 1048592 | tf_op jit(solution)/shard_map/reduce_scatter | solution.py:51
  284.9 1.3 slice_bitcast_fusion
  286.2 1.0 copy.17
  287.1 1.0 copy.18
  288.1 146.3 %reduce-scatter.3.cloned.1.call-done = f32[512,2048]{1,0:T(8,128)} async-done(((f32[512,8192]{1,0:T(8,128)}), f32[512,2048]{1,0:T(8,128)}) %reduce-scatter.3.cloned.1.call-update) | async-done | bytes 4194320 | tf_op jit(solution)/shard_map/reduce_scatter | solution.py:48
  434.4 3.8 convert_bitcast_fusion
  (13 shorter events, 0.0 us)
Async XLA Ops:
  8.0 47.5 %all-gather.5.cloned.1.call-start = ((), (), s32[]{:S(2)}) async-start(), calls=%async_computation.5 | async-start | bytes 4456448 | tf_op jit(solution)/shard_map/all_gather | solution.py:38
  8.7 88.6 %all-gather.7.cloned.1.call-start = ((), (), s32[]{:S(2)}) async-start(), calls=%async_computation.6 | async-start | bytes 4456448 | tf_op jit(solution)/shard_map/all_gather | solution.py:44
  9.5 106.4 %all-reduce.2.cloned.1.call-start = ((), (), s32[]{:S(2)}) async-start(), calls=%async_computation.4 | async-start | bytes 524288 | tf_op jit(solution)/shard_map/psum | solution.py:67
  11.3 273.5 %reduce-scatter.5.cloned.1.call-start = ((), (), s32[]{:S(2)}) async-start(), calls=%async_computation.3 | async-start | bytes 17825792 | tf_op jit(solution)/shard_map/reduce_scatter | solution.py:51
  25.3 30.2 %copy-start.2 = (bf16[1,512,256]{2,1,0:T(8,128)(2,1)S(1)}, bf16[1,512,256]{2,1,0:T(8,128)(2,1)}, u32[]{:S(2)}) copy-start(bf16[1,512,256]{2,1,0:T(8,128)(2,1)} %param.12) | copy-start | bytes 786436
  25.3 72.0 %copy-start.1 = (bf16[1,512,256]{2,1,0:T(8,128)(2,1)S(1)}, bf16[1,512,256]{2,1,0:T(8,128)(2,1)}, u32[]{:S(2)}) copy-start(bf16[1,512,256]{2,1,0:T(8,128)(2,1)} %param.13) | copy-start | bytes 786436
  25.3 409.1 %reduce-scatter.3.cloned.1.call-start = ((), (), s32[]{:S(2)}) async-start(), calls=%async_computation.2 | async-start | bytes 20971520 | tf_op jit(solution)/shard_map/reduce_scatter | solution.py:48
  113.1 1.5 copy-start.5
  113.1 2.7 copy-start
  113.1 2.8 copy-start.3
  113.1 2.8 copy-start.4
Sparse Core Ops, SparseCore 0:
  10.7 44.7 all-gather.4
  57.3 39.9 all-gather.6
  99.9 184.9 reduce-scatter.4
  287.3 147.0 reduce-scatter.2
Sparse Core Ops, SparseCore 1:
  13.3 56.2 all-reduce.1
where the time goes:
time: 448 us; the launch traced here: 445 us
  waiting for transfers between devices  376 us (84%)
  matrix products  40 us (9%)
  between operations  17.3 us (4%)
  other arithmetic  8.45 us (2%)
    reduce_scatter x1, waiting for transfers between devices, local(): lax.psum_scatter(lax.dot_general(tokens_in, both_grad, (((0,), (0,)), (()...  167 us
    reduce_scatter x1, waiting for transfers between devices, local(): lax.psum_scatter(term, 'tensor', scatter_dimension=1, tiled=True)  146 us
    all_gather x1, waiting for transfers between devices, local(): lax.all_gather(value_weight[0], 'fsdp', axis=0, tiled=True)  31.6 us
    all_gather x1, waiting for transfers between devices, local(): lax.all_gather(key_weight[0], 'fsdp', axis=0, tiled=True)  30.1 us
    dot_general x1, matrix products, local(): lax.dot_general(grad_v, lax.all_gather(value_weight[0], 'fsdp', axis=0, t...  15.8 us
    dot_general x1, matrix products, local(): lax.dot_general(tokens_in, both_grad, (((0,), (0,)), ((), ())), preferred...  13.9 us
    dot_general x1, matrix products, local(): lax.dot_general(grad_k, lax.all_gather(key_weight[0], 'fsdp', axis=0, til...  10.3 us
  transfers between devices with their start and end apart: 5, of which 4 were waited for; matrix products, arithmetic and copies ran while one was open for 11% of the time, Pallas kernels for 0%

commit v1 on v0

v1 whole, which is shorter than its diff:
```python
import jax
import jax.numpy as jnp
from jax import lax
from jax.experimental import pallas as pl
from jax.experimental.pallas import tpu as pltpu
from jax.sharding import Mesh, PartitionSpec as P

WARMUP = 64


momentum_decay = 0.9
mixing = 0.5
bf16 = jnp.bfloat16
f32 = jnp.float32
VMEM_LIMIT = 16 * 1024 * 1024


def shift(a, axis, by):
    n = lax.axis_size(axis)
    return lax.ppermute(a, axis, [(i, (i + by) % n) for i in range(n)])


def outer_step(global_part, momentum_part, average, rate):
    delta = global_part - average
    fresh_momentum = momentum_decay * momentum_part + delta
    fresh_global = global_part - rate * (delta + momentum_decay * fresh_momentum)
    return (fresh_global, fresh_momentum)


fence = lax.optimization_barrier
VMEM_SPEC = pl.BlockSpec(memory_space=pltpu.VMEM)
HBM_SPEC = pl.BlockSpec(memory_space=pltpu.HBM)
SMEM_SPEC = pl.BlockSpec(memory_space=pltpu.SMEM)


def call(kernel, where, ins, outs, scratch=(), far=(), aliases=None, flops=0):
    moved = sum(a.size * a.dtype.itemsize for a in list(ins) + list(outs))
    n_in = len(ins)
    spaces = [pltpu.HBM if k in far else pltpu.VMEM for k in range(n_in + len(outs))]
    specs = [HBM_SPEC if space is pltpu.HBM else VMEM_SPEC for space in spaces]
    placed = [pltpu.with_memory_space_constraint(a, space) for a, space in zip(ins, spaces)]
    return pl.pallas_call(
        kernel,
        out_shape=[space(a.shape, a.dtype) for a, space in zip(outs, spaces[n_in:])],
        in_specs=[SMEM_SPEC] + specs[:n_in],
        out_specs=specs[n_in:],
        scratch_shapes=list(scratch),
        input_output_aliases=aliases or {},
        compiler_params=pltpu.CompilerParams(vmem_limit_bytes=VMEM_LIMIT),
        cost_estimate=pl.CostEstimate(flops=flops, bytes_accessed=moved, transcendentals=0),
    )(where, *placed)


def like(*shape, dtype=bf16):
    return jax.ShapeDtypeStruct(shape, dtype)


def started(src, dst, sem):
    copy = pltpu.make_async_copy(src, dst, sem)
    copy.start()
    return copy


def column(ref, index, width):
    return ref.at[:, pl.ds(pl.multiple_of(index * width, width), width)]


def join_kernel(_, a, b, out, sems):
    width = a.shape[1]
    copies = [started(a, out.at[:, :width], sems.at[0]), started(b, out.at[:, width:], sems.at[1])]
    for copy in copies:
        copy.wait()


def join(none, a, b):
    rows, width = a.shape
    return call(join_kernel, none, [a, b], [like(rows, 2 * width)], [pltpu.SemaphoreType.DMA((2,))], far=(0, 1))[0]


def pack_kernel(where, x, grads, out, sems):
    width = out.shape[2]
    copies = [started(column(x, where[i], width), out.at[i], sems.at[i]) for i in range(8)]
    out[8] = grads[...]
    for copy in copies:
        copy.wait()


def pack_columns(where, tokens_in, grads):
    rows, width = grads.shape
    return call(
        pack_kernel, where, [tokens_in, grads], [like(9, rows, width)], [pltpu.SemaphoreType.DMA((8,))], far=(0,)
    )[0]


def partial_kernel(where, x, grads, pack, up, down, far, own, x_buf, sems):
    width = grads.shape[1]

    def load(i):
        return started(column(x, where[i], width), x_buf.at[i % 3], sems.at[i % 3])

    loads = [load(0), load(1)]
    for i in range(8):
        if i < 6:
            loads.append(load(i + 2))
        loads[i].wait()
        acc = lax.dot_general(grads[...], x_buf[i % 3], (((0,), (0,)), ((), ())), preferred_element_type=f32)
        acc = acc + lax.dot_general(pack[8], pack[i], (((0,), (0,)), ((), ())), preferred_element_type=f32)
        (up, down, far, own)[i // 2][i % 2] = acc.astype(bf16)


def partials(where, tokens_in, grads, pack):
    rows, width = grads.shape
    return call(
        partial_kernel,
        where,
        [tokens_in, grads, pack],
        [like(2, width, width)] * 4,
        [pltpu.VMEM((3, rows, width), bf16), pltpu.SemaphoreType.DMA((3,))],
        far=(0,),
        flops=32 * rows * width * width,
    )


def pick_kernel(where, *refs):
    held, outs = refs[:4], refs[4:]
    for s in range(4):
        for d in range(4):
            @pl.when((where[0] + s) % 4 == d)
            def _(s=s, d=d):
                outs[s][...] = held[d][...]


def pick(turn, held):
    return call(pick_kernel, turn, held, [like(*held[0].shape)] * 4)


def back_kernel(where, *refs):
    heads, heads_sib, weights, (out, sib_out, o_buf, sem) = refs[:4], refs[4:8], refs[8:12], refs[-4:]
    width = o_buf.shape[1]

    def product(lhs):
        acc = None
        for g, w in zip(lhs, weights):
            part = lax.dot_general(g[...], w[...], (((1,), (1,)), ((), ())), preferred_element_type=f32)
            acc = part if acc is None else acc + part
        return acc.astype(bf16)

    o_buf[...] = product(heads)
    kept = started(o_buf, column(out, where[0], width), sem)
    sib_out[...] = product(heads_sib)
    kept.wait()


def back_block(where, heads, heads_sib, weights, so_far):
    tokens, width = heads[0].shape
    ins = [*heads, *heads_sib, *weights] + ([] if so_far is None else [so_far])
    n = len(ins)
    return call(
        back_kernel,
        where,
        ins,
        [like(tokens, 4 * width), like(tokens, width)],
        [pltpu.VMEM((tokens, width), bf16), pltpu.SemaphoreType.DMA],
        far=(12, n),
        aliases={} if so_far is None else {13: 0},
        flops=16 * tokens * width * width,
    )


def place_kernel(where, a, b, _, out, sems):
    width = a.shape[1]
    copies = [started(src, column(out, where[k], width), sems.at[k]) for k, src in enumerate((a, b))]
    for copy in copies:
        copy.wait()


def place(where, a, b, back):
    return call(
        place_kernel, where, [a, b, back], [like(*back.shape)], [pltpu.SemaphoreType.DMA((2,))], far=(2, 3), aliases={3: 0}
    )[0]


def other_kernel(_, a, b, c, d, out):
    out[...] = (a[0].astype(f32) + b[0].astype(f32) + c[0].astype(f32) + d[0].astype(f32)).astype(bf16)


def other_sum(none, parts):
    return call(other_kernel, none, parts, [like(*parts[0].shape[1:])])[0]


def mine_kernel(_, a, b, c, d, e, key_out, value_out, k_buf, v_buf, sems):
    width = k_buf.shape[1]

    def total(rows):
        return sum(ref[1, rows].astype(f32) for ref in (a, b, c, d)) + e[rows].astype(f32)

    k_buf[...] = total(slice(0, width)).T
    first = started(k_buf, key_out, sems.at[0])
    v_buf[...] = total(slice(width, 2 * width)).T
    started(v_buf, value_out, sems.at[1]).wait()
    first.wait()


def mine_sum(none, parts, received):
    _, rows, cols = parts[0].shape
    half = (cols, rows // 2)
    return call(
        mine_kernel,
        none,
        [*parts, received],
        [like(*half, dtype=f32)] * 2,
        [pltpu.VMEM(half, f32), pltpu.VMEM(half, f32), pltpu.SemaphoreType.DMA((2,))],
        far=(5, 6),
    )


def local(
    inputs,
    key_grad,
    value_grad,
    key_weight,
    value_weight,
    global_params,
    momentum,
    local_params,
    fragment,
    step,
    outer_rates,
):
    iy, iz, ic, ix = (lax.axis_index(a).astype(jnp.int32) for a in ("y", "z", "c", "x"))
    none = jnp.zeros((1,), jnp.int32)
    tokens_in = inputs[0]
    base = jnp.stack([((iy + d) % 4) * 4 + z * 2 for d in (1, 3, 2, 0) for z in (1 - iz, iz)])
    local_now = local_params[0]
    sent = local_now.astype(bf16)

    weight = join(none, key_weight[0], value_weight[0])
    w1, w3 = shift(weight, "y", -1), shift(weight, "y", -3)
    grads = join(none, key_grad[0], value_grad[0])
    pack = shift(pack_columns(base + 1 - ic, tokens_in, grads), "c", 1)
    r1, r3 = shift(sent, "r", 1), shift(sent, "r", 3)

    pack, sent_b, grads_b, w1, w3, weight_b = fence((pack, sent, grads, w1, w3, weight))
    parts = partials(base + ic, tokens_in, grads, pack)
    grads_sib = pack[8]
    w2 = shift(weight_b, "y", 2)
    h1, h3 = shift(grads_b, "x", 1), shift(grads_b, "x", 3)
    r2 = shift(sent_b, "r", 2)

    w2, w1, w3, parts, h1, h3, r1, r2, r3 = fence((w2, w1, w3, parts, h1, h3, r1, r2, r3))
    near0, pick1, pick2, pick3 = pick(((ix - iy) % 4).reshape(1), [weight, w1, w2, w3])
    near1, near3 = shift(pick1, "x", 1), shift(pick3, "x", 3)
    over0 = shift(near0, "z", 1)
    up, down, far, own = parts
    up, down = shift(up, "y", 1), shift(down, "y", 3)

    near1, near3, over0, pick2, h1 = fence((near1, near3, over0, pick2, h1))
    near2 = shift(pick2, "x", 2)
    over1 = shift(near1, "z", 1)
    h1c = shift(h1, "c", 1)

    near2, over1, up, down, h1c, grads_f, h3, near3, far = fence((near2, over1, up, down, h1c, grads, h3, near3, far))
    over3 = shift(near3, "z", 1)
    far = shift(far, "y", 2)
    h2 = shift(grads_f, "x", 2)
    h3c = shift(h3, "c", 1)

    over3, h2, h3c, near2 = fence((over3, h2, h3c, near2))
    over2 = shift(near2, "z", 1)
    h2c = shift(h2, "c", 1)
    heads, heads_sib = [grads, h1, h2, h3], [grads_sib, h1c, h2c, h3c]
    back, near_out = back_block((iz * 2 + ic).reshape(1), heads, heads_sib, [near0, near1, near2, near3], None)

    over2, far, back, near_out = fence((over2, far, back, near_out))
    parts = [up, down, far, own]
    received = shift(other_sum(none, parts), "z", 1)
    near_out = shift(near_out, "c", 1)
    back, over_out = back_block(((1 - iz) * 2 + ic).reshape(1), heads, heads_sib, [over0, over1, over2, over3], back)
    over_out = shift(over_out, "c", 1)
    back = place(jnp.stack([iz * 2 + 1 - ic, (1 - iz) * 2 + 1 - ic]), near_out, over_out, back)
    wgrad_k, wgrad_v = mine_sum(none, parts, received)

    total = sent.astype(f32) + r1.astype(f32) + r2.astype(f32) + r3.astype(f32)
    count_frag = outer_rates.shape[0]
    chosen = (jnp.arange(count_frag, dtype=jnp.int32) == fragment[0]).astype(f32)
    warm = jnp.minimum(1.0, (step[0].astype(f32) + 1.0) / WARMUP)
    rate = jnp.sum(chosen * outer_rates) * warm
    replicas = lax.axis_size("r")
    fresh_global, fresh_momentum = outer_step(global_params, momentum, total / replicas, rate)
    fresh_local = mixing * local_now + (1.0 - mixing) * fresh_global
    return (
        back[None],
        wgrad_k[None],
        wgrad_v[None],
        fresh_global,
        fresh_momentum,
        fresh_local[None],
    )


def solution(mesh):
    fine = Mesh(mesh.devices.reshape(4, 4, 2, 2, 4), ("r", "y", "z", "c", "x"))
    fsdp = ("y", "z", "c")
    split = P("r", fsdp, "x")
    in_specs = (
        P("r", fsdp, None),
        split,
        split,
        split,
        split,
        P(fsdp, "x"),
        P(fsdp, "x"),
        split,
        P(),
        P(),
        P(),
    )
    out_specs = (split, split, split, P(fsdp, "x"), P(fsdp, "x"), split)
    return jax.shard_map(local, mesh=fine, in_specs=in_specs, out_specs=out_specs, check_vma=False)
```

time: 448 us -> 144 us (0.32)
  the two profiles are of different devices: /device:TPU:6 before, /device:TPU:64 now
where the time goes in v1:
time: 144 us; the launch traced here: 143 us
  waiting for transfers between devices  52 us (36%)
  starting transfers between devices  30.2 us (21%)
  Pallas kernels  29.8 us (21%)
  local copies, waits for them, and re-layouts  23.9 us (17%)
  other arithmetic  4.36 us (3%)
  between operations  3.1 us (2%)
    ppermute x26, waiting for transfers between devices, shift(): return lax.ppermute(a, axis, [(i, (i + by) % n) for i in range(n)])  52 us
    ppermute x26, starting transfers between devices, shift(): return lax.ppermute(a, axis, [(i, (i + by) % n) for i in range(n)])  30.2 us
    pallas_call x10, Pallas kernels, call(): pl.pallas_call(kernel, out_shape=[space(a.shape, a.dtype) for a, space in...  29.8 us
    unnamed x68, local copies, waits for them, and re-layouts  22.7 us
    broadcast_in_dim x1, other arithmetic, local(): fresh_local[None]  2.92 us
  transfers between devices with their start and end apart: 26, of which 9 were waited for; matrix products, arithmetic and copies ran while one was open for 4% of the time, Pallas kernels for 15%

profile of v1, /device:TPU:64, one launch (start us, length us, event | category | flops | bytes accessed | tf_op | source)
XLA Modules:
  0.0 143.4 jit_solution(17912844969052356083)
XLA Ops:
  1.8 2.8 %shard_map.156 = bf16[9,512,512]{2,1,0:T(8,128)(2,1)S(1)} custom-call(s32[8]{0:T(128)S(1)} %get-tuple-element.118.where, bf16[512,8192]{1,0:T(8,128)(2,1)} %bitcast.37, bf16[512,512]{1,0:T(8,128)(2,1)S(1)} %shard_map.155.grads.refs_0_), custom_call_target="tpu_custom_call" | custom-call | bytes 13631488 | tf_op jit(solution)/shard_map/pallas_call | solution.py:42
  11.2 10.2 %collective-permute-done.2.refs_3_ = bf16[512,512]{1,0:T(8,128)(2,1)S(1)} collective-permute-done((bf16[512,512]{1,0:T(8,128)(2,1)S(1)}, bf16[512,512]{1,0:T(8,128)(2,1)S(1)}, u32[]{:S(2)}, u32[]{:S(2)}) %collective-permute-start.2) | collective-permute-done | bytes 524320 | tf_op jit(solution)/shard_map/ppermute | solution.py:20
  23.1 2.2 %copy-done.21 = bf16[9,512,512]{2,1,0:T(8,128)(2,1)} copy-done((bf16[9,512,512]{2,1,0:T(8,128)(2,1)}, bf16[9,512,512]{2,1,0:T(8,128)(2,1)S(1)}, u32[]{:S(2)}) %copy-start.21) | copy-done | bytes 4718616
  25.2 2.1 %collective-permute-start.3 = (bf16[512,512]{1,0:T(8,128)(2,1)S(1)}, bf16[512,512]{1,0:T(8,128)(2,1)}, u32[]{:S(2)}, u32[]{:S(2)}) collective-permute-start(bf16[512,512]{1,0:T(8,128)(2,1)S(1)} %shard_map.154.refs_0_), channel_id=1, source_target_pairs={{0,32},{16,48},{32,0},{48,16},{1,33},{17,49},{33,1},{49,17},{2,34}... | collective-permute-start | bytes 1572872 | tf_op jit(solution)/shard_map/ppermute | solution.py:20
  27.4 2.8 %collective-permute-start.5 = (bf16[512,512]{1,0:T(8,128)(2,1)S(1)}, bf16[512,512]{1,0:T(8,128)(2,1)S(1)}, u32[]{:S(2)}, u32[]{:S(2)}) collective-permute-start(bf16[512,512]{1,0:T(8,128)(2,1)S(1)} %shard_map.155.grads.refs_0_), channel_id=1, source_target_pairs={{0,3},{1,0},{2,1},{3,2},{4,7},{5,4},{6,5},{7,6},{8,11},{9,8},{10,9... | collective-permute-start | bytes 1572872 | tf_op jit(solution)/shard_map/ppermute | solution.py:20
  30.1 4.5 %collective-permute-start.6 = (bf16[64,2048]{1,0:T(8,128)(2,1)}, bf16[64,2048]{1,0:T(8,128)(2,1)}, u32[]{:S(2)}, u32[]{:S(2)}) collective-permute-start(bf16[64,2048]{1,0:T(8,128)(2,1)} %bitcast_convert_fusion), channel_id=1, source_target_pairs={{0,64},{64,128},{128,192},{192,0},{1,65},{65,129},{129,193},{193,1... | collective-permute-start | bytes 786440 | tf_op jit(solution)/shard_map/ppermute | solution.py:20
  35.6 2.3 %copy-done.22 = bf16[9,512,512]{2,1,0:T(8,128)(2,1)S(1)} copy-done((bf16[9,512,512]{2,1,0:T(8,128)(2,1)S(1)}, bf16[9,512,512]{2,1,0:T(8,128)(2,1)}, u32[]{:S(2)}) %copy-start.22) | copy-done | bytes 4718616
  38.0 7.9 %shard_map.157 = (bf16[2,512,512]{2,1,0:T(8,128)(2,1)S(1)}, bf16[2,512,512]{2,1,0:T(8,128)(2,1)S(1)}, bf16[2,512,512]{2,1,0:T(8,128)(2,1)}, bf16[2,512,512]{2,1,0:T(8,128)(2,1)S(1)}) custom-call(s32[8]{0:T(128)S(1)} %get-tuple-element.117.where, bf16[512,8192]{1,0:T(8,128)(2,1)} %bitcast.38, bf16[512,512]{1,0:T(8,128)(2,1)S(1)} %shard_map.155.grads.refs_0_, ...), custom_call_target="tpu_custom_call" | custom-call | flops 4294967296 | bytes 17825792 | tf_op jit(solution)/shard_map/pallas_call | solution.py:42
  45.8 6.4 %collective-permute-done.6 = bf16[64,2048]{1,0:T(8,128)(2,1)} collective-permute-done((bf16[64,2048]{1,0:T(8,128)(2,1)}, bf16[64,2048]{1,0:T(8,128)(2,1)}, u32[]{:S(2)}, u32[]{:S(2)}) %collective-permute-start.6) | collective-permute-done | bytes 262176 | tf_op jit(solution)/shard_map/ppermute | solution.py:20
  52.2 5.8 %collective-permute-done.7 = bf16[64,2048]{1,0:T(8,128)(2,1)S(1)} collective-permute-done((bf16[64,2048]{1,0:T(8,128)(2,1)}, bf16[64,2048]{1,0:T(8,128)(2,1)S(1)}, u32[]{:S(2)}, u32[]{:S(2)}) %collective-permute-start.7) | collective-permute-done | bytes 262176 | tf_op jit(solution)/shard_map/ppermute | solution.py:20
  60.7 2.8 %collective-permute-start.10 = (bf16[512,512]{1,0:T(8,128)(2,1)S(1)}, bf16[512,512]{1,0:T(8,128)(2,1)S(1)}, u32[]{:S(2)}, u32[]{:S(2)}) collective-permute-start(bf16[512,512]{1,0:T(8,128)(2,1)S(1)} %get-tuple-element.74), channel_id=1, source_target_pairs={{0,3},{1,0},{2,1},{3,2},{4,7},{5,4},{6,5},{7,6},{8,11},{9,8},{10,9... | collective-permute-start | bytes 1572872 | tf_op jit(solution)/shard_map/ppermute | solution.py:20
  65.2 2.3 %collective-permute-start.15 = (bf16[2,512,512]{2,1,0:T(8,128)(2,1)S(1)}, bf16[2,512,512]{2,1,0:T(8,128)(2,1)S(1)}, u32[]{:S(2)}, u32[]{:S(2)}) collective-permute-start(bf16[2,512,512]{2,1,0:T(8,128)(2,1)S(1)} %get-tuple-element.81), channel_id=1, source_target_pairs={{0,48},{16,0},{32,16},{48,32},{1,49},{17,1},{33,17},{49,33},{2,50}... | collective-permute-start | bytes 3145736 | tf_op jit(solution)/shard_map/ppermute | solution.py:20
  67.5 6.1 %collective-permute-done.9.refs_9_ = bf16[512,512]{1,0:T(8,128)(2,1)S(1)} collective-permute-done((bf16[512,512]{1,0:T(8,128)(2,1)S(1)}, bf16[512,512]{1,0:T(8,128)(2,1)S(1)}, u32[]{:S(2)}, u32[]{:S(2)}) %collective-permute-start.9) | collective-permute-done | bytes 524320 | tf_op jit(solution)/shard_map/ppermute | solution.py:20
  78.4 10.2 %collective-permute-done.12.refs_10_ = bf16[512,512]{1,0:T(8,128)(2,1)S(1)} collective-permute-done((bf16[512,512]{1,0:T(8,128)(2,1)S(1)}, bf16[512,512]{1,0:T(8,128)(2,1)S(1)}, u32[]{:S(2)}, u32[]{:S(2)}) %collective-permute-start.12) | collective-permute-done | bytes 524320 | tf_op jit(solution)/shard_map/ppermute | solution.py:20
  91.2 1.7 %collective-permute-start.18 = (bf16[512,512]{1,0:T(8,128)(2,1)S(1)}, bf16[512,512]{1,0:T(8,128)(2,1)}, u32[]{:S(2)}, u32[]{:S(2)}) collective-permute-start(bf16[512,512]{1,0:T(8,128)(2,1)S(1)} %shard_map.155.grads.refs_0_), channel_id=1, source_target_pairs={{0,2},{1,3},{2,0},{3,1},{4,6},{5,7},{6,4},{7,5},{8,10},{9,11},{10,... | collective-permute-start | bytes 1572872 | tf_op jit(solution)/shard_map/ppermute | solution.py:20
  94.2 1.7 %collective-permute-start.21 = (bf16[2,512,512]{2,1,0:T(8,128)(2,1)}, bf16[2,512,512]{2,1,0:T(8,128)(2,1)}, u32[]{:S(2)}, u32[]{:S(2)}) collective-permute-start(bf16[2,512,512]{2,1,0:T(8,128)(2,1)} %get-tuple-element.91), channel_id=1, source_target_pairs={{0,32},{16,48},{32,0},{48,16},{1,33},{17,49},{33,1},{49,17},{2,34}... | collective-permute-start | bytes 3145736 | tf_op jit(solution)/shard_map/ppermute | solution.py:20
  96.0 6.8 %collective-permute-done.18.refs_2_ = bf16[512,512]{1,0:T(8,128)(2,1)} collective-permute-done((bf16[512,512]{1,0:T(8,128)(2,1)S(1)}, bf16[512,512]{1,0:T(8,128)(2,1)}, u32[]{:S(2)}, u32[]{:S(2)}) %collective-permute-start.18) | collective-permute-done | bytes 524320 | tf_op jit(solution)/shard_map/ppermute | solution.py:20
  115.1 4.7 %shard_map.159 = (bf16[512,2048]{1,0:T(8,128)(2,1)}, bf16[512,512]{1,0:T(8,128)(2,1)}) custom-call(s32[1]{0:T(128)} %bitcast.17.where, bf16[512,512]{1,0:T(8,128)(2,1)S(1)} %shard_map.155.grads.refs_0_, bf16[512,512]{1,0:T(8,128)(2,1)S(1)} %copy-done.4, bf16[512,512]{1,0:T(8,128)(2,1)} %collective-permute-done.18.refs_2_, ...), custom_call_target="tpu_custom_call" | custom-call | flops 2147483648 | bytes 8912896 | tf_op jit(solution)/shard_map/pallas_call | solution.py:42
  119.8 1.8 %collective-permute-done.21.c = bf16[2,512,512]{2,1,0:T(8,128)(2,1)} collective-permute-done((bf16[2,512,512]{2,1,0:T(8,128)(2,1)}, bf16[2,512,512]{2,1,0:T(8,128)(2,1)}, u32[]{:S(2)}, u32[]{:S(2)}) %collective-permute-start.21) | collective-permute-done | bytes 1048608 | tf_op jit(solution)/shard_map/ppermute | solution.py:20
  121.6 2.3 %shard_map.162 = bf16[512,512]{1,0:T(8,128)(2,1)} custom-call(s32[1]{0:T(128)} %constant.72.clone.1._, bf16[2,512,512]{2,1,0:T(8,128)(2,1)S(1)} %collective-permute-done.14.a, bf16[2,512,512]{2,1,0:T(8,128)(2,1)S(1)} %copy-done.1, bf16[2,512,512]{2,1,0:T(8,128)(2,1)} %collective-permute-done.21.c, bf16[2,512,512]{2,1,0:T(8,128)(2,1)S(1)} %get-tuple-element.108.d), custom_call_target="tpu_custom_call" | custom-call | bytes 4718592 | tf_op jit(solution)/shard_map/pallas_call | solution.py:42
  125.4 4.6 %shard_map.160 = (bf16[512,2048]{1,0:T(8,128)(2,1)}, bf16[512,512]{1,0:T(8,128)(2,1)}) custom-call(s32[1]{0:T(128)} %bitcast.19.where, bf16[512,512]{1,0:T(8,128)(2,1)S(1)} %shard_map.155.grads.refs_0_, bf16[512,512]{1,0:T(8,128)(2,1)S(1)} %copy-done.4, bf16[512,512]{1,0:T(8,128)(2,1)} %collective-permute-done.18.refs_2_, ...), custom_call_target="tpu_custom_call", output_to_operand_aliasing={{0}: (13, {})} | custom-call | flops 2147483648 | bytes 11010048 | tf_op jit(solution)/shard_map/pallas_call | solution.py:42
  131.9 2.9 %fusion.1 = (f32[1,64,2048]{2,1,0:T(8,128)}, f32[64,2048]{1,0:T(8,128)}, f32[64,2048]{1,0:T(8,128)}) fusion(f32[1,64,2048]{2,1,0:T(8,128)} %param.18, f32[64,2048]{1,0:T(8,128)} %param.16, bf16[64,2048]{1,0:T(8,128)(2,1)S(1)} %collective-permute-done.8, bf16[64,2048]{1,0:T(8,128)(2,1)} %copy-done.32, bf16[64,2048]{1,0:T(8,128)(2,1)} %collective-permute-done.6, ...), kind=kLoop, calls=%fused_computation.3 | loop fusion | flops 2359296 | bytes 3932164 | tf_op jit(solution)/shard_map/broadcast_in_dim | solution.py:297
  134.8 2.9 %collective-permute-done.25.e = bf16[512,512]{1,0:T(8,128)(2,1)} collective-permute-done((bf16[512,512]{1,0:T(8,128)(2,1)}, bf16[512,512]{1,0:T(8,128)(2,1)}, u32[]{:S(2)}, u32[]{:S(2)}) %collective-permute-start.25) | collective-permute-done | bytes 524320 | tf_op jit(solution)/shard_map/ppermute | solution.py:20
  139.0 2.6 %shard_map.163 = (f32[512,256]{1,0:T(8,128)}, f32[512,256]{1,0:T(8,128)}) custom-call(s32[1]{0:T(128)} %constant.72.clone.1._, bf16[2,512,512]{2,1,0:T(8,128)(2,1)S(1)} %collective-permute-done.14.a, bf16[2,512,512]{2,1,0:T(8,128)(2,1)S(1)} %copy-done.2, bf16[2,512,512]{2,1,0:T(8,128)(2,1)} %collective-permute-done.21.c, ...), custom_call_target="tpu_custom_call" | custom-call | bytes 5767168 | tf_op jit(solution)/shard_map/pallas_call | solution.py:42
  (113 shorter events, 39.9 us)
Async XLA Ops:
  4.6 18.4 %collective-permute-start = (bf16[9,512,512]{2,1,0:T(8,128)(2,1)S(1)}, bf16[9,512,512]{2,1,0:T(8,128)(2,1)S(1)}, u32[]{:S(2)}, u32[]{:S(2)}) collective-permute-start(bf16[9,512,512]{2,1,0:T(8,128)(2,1)S(1)} %shard_map.156), channel_id=1, source_target_pairs={{0,4},{4,0},{1,5},{5,1},{2,6},{6,2},{3,7},{7,3},{8,12},{12,8},{9,1... | collective-permute-start | bytes 14155784 | tf_op jit(solution)/shard_map/ppermute | solution.py:20
  5.8 15.7 %collective-permute-start.2 = (bf16[512,512]{1,0:T(8,128)(2,1)S(1)}, bf16[512,512]{1,0:T(8,128)(2,1)S(1)}, u32[]{:S(2)}, u32[]{:S(2)}) collective-permute-start(bf16[512,512]{1,0:T(8,128)(2,1)S(1)} %shard_map.154.refs_0_), channel_id=1, source_target_pairs={{0,16},{16,32},{32,48},{48,0},{1,17},{17,33},{33,49},{49,1},{2,18}... | collective-permute-start | bytes 1572872 | tf_op jit(solution)/shard_map/ppermute | solution.py:20
  7.5 14.8 %collective-permute-start.1 = (bf16[512,512]{1,0:T(8,128)(2,1)S(1)}, bf16[512,512]{1,0:T(8,128)(2,1)S(1)}, u32[]{:S(2)}, u32[]{:S(2)}) collective-permute-start(bf16[512,512]{1,0:T(8,128)(2,1)S(1)} %shard_map.154.refs_0_), channel_id=1, source_target_pairs={{0,48},{16,0},{32,16},{48,32},{1,49},{17,1},{33,17},{49,33},{2,50}... | collective-permute-start | bytes 1572872 | tf_op jit(solution)/shard_map/ppermute | solution.py:20
  9.9 24.8 %collective-permute-start.8 = (bf16[64,2048]{1,0:T(8,128)(2,1)}, bf16[64,2048]{1,0:T(8,128)(2,1)S(1)}, u32[]{:S(2)}, u32[]{:S(2)}) collective-permute-start(bf16[64,2048]{1,0:T(8,128)(2,1)} %bitcast_convert_fusion), channel_id=1, source_target_pairs={{0,192},{64,0},{128,64},{192,128},{1,193},{65,1},{129,65},{193,129... | collective-permute-start | bytes 786440 | tf_op jit(solution)/shard_map/ppermute | solution.py:20
  25.2 32.8 %collective-permute-start.3 = (bf16[512,512]{1,0:T(8,128)(2,1)S(1)}, bf16[512,512]{1,0:T(8,128)(2,1)}, u32[]{:S(2)}, u32[]{:S(2)}) collective-permute-start(bf16[512,512]{1,0:T(8,128)(2,1)S(1)} %shard_map.154.refs_0_), channel_id=1, source_target_pairs={{0,32},{16,48},{32,0},{48,16},{1,33},{17,49},{33,1},{49,17},{2,34}... | collective-permute-start | bytes 1572872 | tf_op jit(solution)/shard_map/ppermute | solution.py:20
  27.4 30.7 %collective-permute-start.5 = (bf16[512,512]{1,0:T(8,128)(2,1)S(1)}, bf16[512,512]{1,0:T(8,128)(2,1)S(1)}, u32[]{:S(2)}, u32[]{:S(2)}) collective-permute-start(bf16[512,512]{1,0:T(8,128)(2,1)S(1)} %shard_map.155.grads.refs_0_), channel_id=1, source_target_pairs={{0,3},{1,0},{2,1},{3,2},{4,7},{5,4},{6,5},{7,6},{8,11},{9,8},{10,9... | collective-permute-start | bytes 1572872 | tf_op jit(solution)/shard_map/ppermute | solution.py:20
  30.1 27.9 %collective-permute-start.4 = (bf16[512,512]{1,0:T(8,128)(2,1)S(1)}, bf16[512,512]{1,0:T(8,128)(2,1)S(1)}, u32[]{:S(2)}, u32[]{:S(2)}) collective-permute-start(bf16[512,512]{1,0:T(8,128)(2,1)S(1)} %shard_map.155.grads.refs_0_), channel_id=1, source_target_pairs={{0,1},{1,2},{2,3},{3,0},{4,5},{5,6},{6,7},{7,4},{8,9},{9,10},{10,1... | collective-permute-start | bytes 1572872 | tf_op jit(solution)/shard_map/ppermute | solution.py:20
  30.1 22.1 %collective-permute-start.6 = (bf16[64,2048]{1,0:T(8,128)(2,1)}, bf16[64,2048]{1,0:T(8,128)(2,1)}, u32[]{:S(2)}, u32[]{:S(2)}) collective-permute-start(bf16[64,2048]{1,0:T(8,128)(2,1)} %bitcast_convert_fusion), channel_id=1, source_target_pairs={{0,64},{64,128},{128,192},{192,0},{1,65},{65,129},{129,193},{193,1... | collective-permute-start | bytes 786440 | tf_op jit(solution)/shard_map/ppermute | solution.py:20
  34.6 23.4 %collective-permute-start.7 = (bf16[64,2048]{1,0:T(8,128)(2,1)}, bf16[64,2048]{1,0:T(8,128)(2,1)S(1)}, u32[]{:S(2)}, u32[]{:S(2)}) collective-permute-start(bf16[64,2048]{1,0:T(8,128)(2,1)} %bitcast_convert_fusion), channel_id=1, source_target_pairs={{0,128},{64,192},{128,0},{192,64},{1,129},{65,193},{129,1},{193,65... | collective-permute-start | bytes 786440 | tf_op jit(solution)/shard_map/ppermute | solution.py:20
  60.1 13.5 %collective-permute-start.9 = (bf16[512,512]{1,0:T(8,128)(2,1)S(1)}, bf16[512,512]{1,0:T(8,128)(2,1)S(1)}, u32[]{:S(2)}, u32[]{:S(2)}) collective-permute-start(bf16[512,512]{1,0:T(8,128)(2,1)S(1)} %get-tuple-element.73), channel_id=1, source_target_pairs={{0,1},{1,2},{2,3},{3,0},{4,5},{5,6},{6,7},{7,4},{8,9},{9,10},{10,1... | collective-permute-start | bytes 1572872 | tf_op jit(solution)/shard_map/ppermute | solution.py:20
  60.7 12.9 %collective-permute-start.10 = (bf16[512,512]{1,0:T(8,128)(2,1)S(1)}, bf16[512,512]{1,0:T(8,128)(2,1)S(1)}, u32[]{:S(2)}, u32[]{:S(2)}) collective-permute-start(bf16[512,512]{1,0:T(8,128)(2,1)S(1)} %get-tuple-element.74), channel_id=1, source_target_pairs={{0,3},{1,0},{2,1},{3,2},{4,7},{5,4},{6,5},{7,6},{8,11},{9,8},{10,9... | collective-permute-start | bytes 1572872 | tf_op jit(solution)/shard_map/ppermute | solution.py:20
  63.4 11.9 %collective-permute-start.11 = (bf16[512,512]{1,0:T(8,128)(2,1)S(1)}, bf16[512,512]{1,0:T(8,128)(2,1)S(1)}, u32[]{:S(2)}, u32[]{:S(2)}) collective-permute-start(bf16[512,512]{1,0:T(8,128)(2,1)S(1)} %get-tuple-element.75.refs_8_), channel_id=1, source_target_pairs={{0,8},{8,0},{1,9},{9,1},{2,10},{10,2},{3,11},{11,3},{4,12},{12,4},... | collective-permute-start | bytes 1572872 | tf_op jit(solution)/shard_map/ppermute | solution.py:20
  64.2 25.9 %collective-permute-start.14 = (bf16[2,512,512]{2,1,0:T(8,128)(2,1)S(1)}, bf16[2,512,512]{2,1,0:T(8,128)(2,1)S(1)}, u32[]{:S(2)}, u32[]{:S(2)}) collective-permute-start(bf16[2,512,512]{2,1,0:T(8,128)(2,1)S(1)} %get-tuple-element.80), channel_id=1, source_target_pairs={{0,16},{16,32},{32,48},{48,0},{1,17},{17,33},{33,49},{49,1},{2,18}... | collective-permute-start | bytes 3145736 | tf_op jit(solution)/shard_map/ppermute | solution.py:20
  65.2 25.0 %collective-permute-start.15 = (bf16[2,512,512]{2,1,0:T(8,128)(2,1)S(1)}, bf16[2,512,512]{2,1,0:T(8,128)(2,1)S(1)}, u32[]{:S(2)}, u32[]{:S(2)}) collective-permute-start(bf16[2,512,512]{2,1,0:T(8,128)(2,1)S(1)} %get-tuple-element.81), channel_id=1, source_target_pairs={{0,48},{16,0},{32,16},{48,32},{1,49},{17,1},{33,17},{49,33},{2,50}... | collective-permute-start | bytes 3145736 | tf_op jit(solution)/shard_map/ppermute | solution.py:20
  76.1 12.4 %collective-permute-start.12 = (bf16[512,512]{1,0:T(8,128)(2,1)S(1)}, bf16[512,512]{1,0:T(8,128)(2,1)S(1)}, u32[]{:S(2)}, u32[]{:S(2)}) collective-permute-start(bf16[512,512]{1,0:T(8,128)(2,1)S(1)} %get-tuple-element.78), channel_id=1, source_target_pairs={{0,2},{1,3},{2,0},{3,1},{4,6},{5,7},{6,4},{7,5},{8,10},{9,11},{10,... | collective-permute-start | bytes 1572872 | tf_op jit(solution)/shard_map/ppermute | solution.py:20
  77.3 11.3 %collective-permute-start.13 = (bf16[512,512]{1,0:T(8,128)(2,1)S(1)}, bf16[512,512]{1,0:T(8,128)(2,1)S(1)}, u32[]{:S(2)}, u32[]{:S(2)}) collective-permute-start(bf16[512,512]{1,0:T(8,128)(2,1)S(1)} %collective-permute-done.9.refs_9_), channel_id=1, source_target_pairs={{0,8},{8,0},{1,9},{9,1},{2,10},{10,2},{3,11},{11,3},{4,12},{12,4},... | collective-permute-start | bytes 1572872 | tf_op jit(solution)/shard_map/ppermute | solution.py:20
  78.4 11.0 %collective-permute-start.16 = (bf16[512,512]{1,0:T(8,128)(2,1)}, bf16[512,512]{1,0:T(8,128)(2,1)S(1)}, u32[]{:S(2)}, u32[]{:S(2)}) collective-permute-start(bf16[512,512]{1,0:T(8,128)(2,1)} %copy-done.3), channel_id=1, source_target_pairs={{0,4},{4,0},{1,5},{5,1},{2,6},{6,2},{3,7},{7,3},{8,12},{12,8},{9,1... | collective-permute-start | bytes 1572872 | tf_op jit(solution)/shard_map/ppermute | solution.py:20
  91.2 11.6 %collective-permute-start.18 = (bf16[512,512]{1,0:T(8,128)(2,1)S(1)}, bf16[512,512]{1,0:T(8,128)(2,1)}, u32[]{:S(2)}, u32[]{:S(2)}) collective-permute-start(bf16[512,512]{1,0:T(8,128)(2,1)S(1)} %shard_map.155.grads.refs_0_), channel_id=1, source_target_pairs={{0,2},{1,3},{2,0},{3,1},{4,6},{5,7},{6,4},{7,5},{8,10},{9,11},{10,... | collective-permute-start | bytes 1572872 | tf_op jit(solution)/shard_map/ppermute | solution.py:20
  92.9 9.9 %collective-permute-start.17 = (bf16[512,512]{1,0:T(8,128)(2,1)S(1)}, bf16[512,512]{1,0:T(8,128)(2,1)S(1)}, u32[]{:S(2)}, u32[]{:S(2)}) collective-permute-start(bf16[512,512]{1,0:T(8,128)(2,1)S(1)} %collective-permute-done.10.refs_11_), channel_id=1, source_target_pairs={{0,8},{8,0},{1,9},{9,1},{2,10},{10,2},{3,11},{11,3},{4,12},{12,4},... | collective-permute-start | bytes 1572872 | tf_op jit(solution)/shard_map/ppermute | solution.py:20
  94.2 27.4 %collective-permute-start.21 = (bf16[2,512,512]{2,1,0:T(8,128)(2,1)}, bf16[2,512,512]{2,1,0:T(8,128)(2,1)}, u32[]{:S(2)}, u32[]{:S(2)}) collective-permute-start(bf16[2,512,512]{2,1,0:T(8,128)(2,1)} %get-tuple-element.91), channel_id=1, source_target_pairs={{0,32},{16,48},{32,0},{48,16},{1,33},{17,49},{33,1},{49,17},{2,34}... | collective-permute-start | bytes 3145736 | tf_op jit(solution)/shard_map/ppermute | solution.py:20
  105.1 14.7 %collective-permute-start.20 = (bf16[512,512]{1,0:T(8,128)(2,1)}, bf16[512,512]{1,0:T(8,128)(2,1)S(1)}, u32[]{:S(2)}, u32[]{:S(2)}) collective-permute-start(bf16[512,512]{1,0:T(8,128)(2,1)} %copy-done.29), channel_id=1, source_target_pairs={{0,8},{8,0},{1,9},{9,1},{2,10},{10,2},{3,11},{11,3},{4,12},{12,4},... | collective-permute-start | bytes 1572872 | tf_op jit(solution)/shard_map/ppermute | solution.py:20
  123.9 13.9 %collective-permute-start.25 = (bf16[512,512]{1,0:T(8,128)(2,1)}, bf16[512,512]{1,0:T(8,128)(2,1)}, u32[]{:S(2)}, u32[]{:S(2)}) collective-permute-start(bf16[512,512]{1,0:T(8,128)(2,1)} %shard_map.162), channel_id=1, source_target_pairs={{0,8},{8,0},{1,9},{9,1},{2,10},{10,2},{3,11},{11,3},{4,12},{12,4},... | collective-permute-start | bytes 1572872 | tf_op jit(solution)/shard_map/ppermute | solution.py:20
  130.0 11.7 %collective-permute-start.24 = (bf16[512,512]{1,0:T(8,128)(2,1)}, bf16[512,512]{1,0:T(8,128)(2,1)S(1)}, u32[]{:S(2)}, u32[]{:S(2)}) collective-permute-start(bf16[512,512]{1,0:T(8,128)(2,1)} %get-tuple-element.103), channel_id=1, source_target_pairs={{0,4},{4,0},{1,5},{5,1},{2,6},{6,2},{3,7},{7,3},{8,12},{12,8},{9,1... | collective-permute-start | bytes 1572872 | tf_op jit(solution)/shard_map/ppermute | solution.py:20
  130.1 11.6 %collective-permute-start.23 = (bf16[512,512]{1,0:T(8,128)(2,1)}, bf16[512,512]{1,0:T(8,128)(2,1)S(1)}, u32[]{:S(2)}, u32[]{:S(2)}) collective-permute-start(bf16[512,512]{1,0:T(8,128)(2,1)} %get-tuple-element.97), channel_id=1, source_target_pairs={{0,4},{4,0},{1,5},{5,1},{2,6},{6,2},{3,7},{7,3},{8,12},{12,8},{9,1... | collective-permute-start | bytes 1572872 | tf_op jit(solution)/shard_map/ppermute | solution.py:20
  (36 other events, 241.5 us)

commit v2 on v1

v2 whole, which is shorter than its diff:
```python
import jax
import jax.numpy as jnp
from jax import lax
from jax.experimental import pallas as pl
from jax.experimental.pallas import tpu as pltpu
from jax.sharding import Mesh, PartitionSpec as P

WARMUP = 64


momentum_decay = 0.9
mixing = 0.5
bf16 = jnp.bfloat16
f32 = jnp.float32
VMEM_LIMIT = 16 * 1024 * 1024


def shift(a, axis, by):
    n = lax.axis_size(axis)
    return lax.ppermute(a, axis, [(i, (i + by) % n) for i in range(n)])


def outer_step(global_part, momentum_part, average, rate):
    delta = global_part - average
    fresh_momentum = momentum_decay * momentum_part + delta
    fresh_global = global_part - rate * (delta + momentum_decay * fresh_momentum)
    return (fresh_global, fresh_momentum)


fence = lax.optimization_barrier
VMEM_SPEC = pl.BlockSpec(memory_space=pltpu.VMEM)
HBM_SPEC = pl.BlockSpec(memory_space=pltpu.HBM)
SMEM_SPEC = pl.BlockSpec(memory_space=pltpu.SMEM)


def call(kernel, where, ins, outs, scratch=(), far=(), aliases=None, flops=0):
    n_in = len(ins)
    spaces = [pltpu.HBM if k in far else pltpu.VMEM for k in range(n_in + len(outs))]
    specs = [HBM_SPEC if space is pltpu.HBM else VMEM_SPEC for space in spaces]
    placed = [pltpu.with_memory_space_constraint(a, space) for a, space in zip(ins, spaces)]
    return pl.pallas_call(
        kernel,
        out_shape=[space(a.shape, a.dtype) for a, space in zip(outs, spaces[n_in:])],
        in_specs=[SMEM_SPEC] + specs[:n_in],
        out_specs=specs[n_in:],
        scratch_shapes=list(scratch),
        input_output_aliases=aliases or {},
        compiler_params=pltpu.CompilerParams(vmem_limit_bytes=VMEM_LIMIT),
        cost_estimate=pl.CostEstimate(flops=flops, bytes_accessed=0, transcendentals=0),
    )(where, *placed)


def like(*shape, dtype=bf16):
    return jax.ShapeDtypeStruct(shape, dtype)


def started(src, dst, sem):
    copy = pltpu.make_async_copy(src, dst, sem)
    copy.start()
    return copy


def column(ref, index, width):
    return ref.at[:, pl.ds(pl.multiple_of(index * width, width), width)]


def join_kernel(_, a, b, out, sems):
    width = a.shape[1]
    copies = [started(a, out.at[:, :width], sems.at[0]), started(b, out.at[:, width:], sems.at[1])]
    for copy in copies:
        copy.wait()


def join(none, a, b):
    rows, width = a.shape
    return call(join_kernel, none, [a, b], [like(rows, 2 * width)], [pltpu.SemaphoreType.DMA((2,))], far=(0, 1))[0]


def prepare_kernel(where, x, gk, gv, grads, pack, sems):
    width = gk.shape[1]
    block = pack.shape[2]
    count = pack.shape[0] - 1
    joined = [started(gk, grads.at[:, :width], sems.at[0]), started(gv, grads.at[:, width:], sems.at[1])]
    copies = [started(column(x, where[i], block), pack.at[i], sems.at[2 + i]) for i in range(count)]
    for copy in joined:
        copy.wait()
    pack[count] = grads[...]
    for copy in copies:
        copy.wait()


def prepare(where, tokens_in, gk, gv):
    rows, width = gk.shape
    count = where.shape[0]
    outs = [like(rows, 2 * width), like(count + 1, rows, 2 * width)]
    return call(prepare_kernel, where, [tokens_in, gk, gv], outs, [pltpu.SemaphoreType.DMA((2 + count,))], far=(0, 1, 2))


def partial_kernel(where, x, grads, pack, *refs):
    pairs, sib_out, (x_buf, sems) = refs[:-3], refs[-3], refs[-2:]
    width = grads.shape[1]
    outs = [ref.at[k] for ref in pairs for k in range(2)]
    sib = pack.at[len(outs)]

    def load(i):
        return started(column(x, where[i], width), x_buf.at[i % 3], sems.at[i % 3])

    loads = [load(i) for i in range(2)]
    for i, out in enumerate(outs):
        if i + 2 < len(outs):
            loads.append(load(i + 2))
        loads[i].wait()
        acc = lax.dot_general(grads[...], x_buf[i % 3], (((0,), (0,)), ((), ())), preferred_element_type=f32)
        acc = acc + lax.dot_general(sib[...], pack[i], (((0,), (0,)), ((), ())), preferred_element_type=f32)
        out[...] = acc.astype(bf16)
    sib_out[...] = sib[...]


def partials(where, tokens_in, grads, pack):
    rows, width = grads.shape
    return call(
        partial_kernel,
        where,
        [tokens_in, grads, pack],
        [like(2, width, width)] * 4 + [like(rows, width)],
        [pltpu.VMEM((3, rows, width), bf16), pltpu.SemaphoreType.DMA((3,))],
        far=(0,),
        flops=32 * rows * width * width,
    )


def pick_kernel(where, *refs):
    held, outs = refs[:4], refs[4:]
    for s in range(4):
        for d in range(4):
            @pl.when((where[0] + s) % 4 == d)
            def _(s=s, d=d):
                outs[s][...] = held[d][...]


def pick(turn, held):
    return call(pick_kernel, turn, held, [like(*held[0].shape)] * 4)


def product(lhs, rhs):
    return lax.dot_general(lhs[...], rhs[...], (((1,), (1,)), ((), ())), preferred_element_type=f32)


def early_kernel(_, *refs):
    own, sib, weights = refs[0:2], refs[2:4], refs[4:6]
    own_acc, sib_acc, buf, sems = refs[6:]
    order = [group[k] for k in range(2) for group in (weights, own, sib)]
    copies = [started(src, buf.at[i], sems.at[i]) for i, src in enumerate(order)]
    for k in range(2):
        for j, acc in enumerate((None, own_acc, sib_acc)):
            copies[3 * k + j].wait()
            if acc is not None:
                part = product(buf.at[3 * k + j], buf.at[3 * k])
                acc[...] = part if k == 0 else acc[...] + part


def early_slots(none, own, sib, weights):
    tokens, width = own[0].shape
    return call(
        early_kernel,
        none,
        [*own, *sib, *weights],
        [like(tokens, width, dtype=f32)] * 2,
        [pltpu.VMEM((6, tokens, width), bf16), pltpu.SemaphoreType.DMA((6,))],
        far=(0, 1, 2, 4, 5),
        flops=8 * tokens * width * width,
    )


def late_slots(refs, accs, w_buf, a_buf, sems, emit):
    heads, blocks = refs[0:2], (refs[2:4], refs[4:6])
    copies = [
        (started(block[0], w_buf.at[k], sems.at[0, k]), started(acc, a_buf.at[k], sems.at[1, k]))
        for k, (block, acc) in enumerate(zip(blocks, accs))
    ]
    for k, block in enumerate(blocks):
        part = product(heads[1], block[1])
        for copy in copies[k]:
            copy.wait()
        emit(k, (a_buf[k] + product(heads[0], w_buf.at[k]) + part).astype(bf16))


def late_scratch(acc):
    return [pltpu.VMEM((2, *acc.shape), bf16), pltpu.VMEM((2, *acc.shape), f32), pltpu.SemaphoreType.DMA((2, 2))]


def loose_kernel(_, *refs):
    out = refs[8]

    def emit(k, block):
        out[k] = block

    late_slots(refs[:6], refs[6:8], *refs[9:], emit)


def loose_blocks(none, heads, near, over, accs):
    ins = [*heads, *near, *over, *accs]
    return call(loose_kernel, none, ins, [like(2, *accs[0].shape)], late_scratch(accs[0]), far=(2, 4, 6, 7))[0]


def back_kernel(where, *refs):
    out, buf, out_sems = refs[8], refs[9], refs[10]
    copies = []

    def emit(k, block):
        buf[k] = block
        copies.append(started(buf.at[k], column(out, where[k], buf.shape[2]), out_sems.at[k]))

    late_slots(refs[:6], refs[6:8], *refs[11:], emit)
    for copy in copies:
        copy.wait()


def back_blocks(where, heads, near, over, accs):
    tokens, width = accs[0].shape
    ins = [*heads, *near, *over, *accs]
    scratch = [pltpu.VMEM((2, tokens, width), bf16), pltpu.SemaphoreType.DMA((2,))] + late_scratch(accs[0])
    return call(back_kernel, where, ins, [like(tokens, 4 * width)], scratch, far=(2, 4, 6, 7, 8))[0]


def place_kernel(where, blocks, _, out, sems):
    width = blocks.shape[2]
    copies = [started(blocks.at[k], column(out, where[k], width), sems.at[k]) for k in range(2)]
    for copy in copies:
        copy.wait()


def place(where, blocks, back):
    return call(
        place_kernel, where, [blocks, back], [like(*back.shape)], [pltpu.SemaphoreType.DMA((2,))], far=(1, 2), aliases={2: 0}
    )[0]


def relay_kernel(_, rest, up, down, first, second):
    first[...] = (rest[0].astype(f32) + up[0].astype(f32)).astype(bf16)
    second[...] = (rest[1].astype(f32) + down[0].astype(f32)).astype(bf16)


def other_kernel(_, own, up, down, out):
    out[...] = (own[0].astype(f32) + up[...].astype(f32) + down[1].astype(f32)).astype(bf16)


def mine_kernel(_, own, up, down, out):
    out[...] = (own[1].astype(f32) + up[1].astype(f32) + down[...].astype(f32)).T


def final_kernel(_, part, received, key_out, value_out, k_buf, v_buf, sems):
    width = k_buf.shape[1]
    k_buf[...] = part[:, :width] + received[:width].astype(f32).T
    first = started(k_buf, key_out, sems.at[0])
    v_buf[...] = part[:, width:] + received[width:].astype(f32).T
    started(v_buf, value_out, sems.at[1]).wait()
    first.wait()


def final_sum(none, part, received):
    rows, cols = received.shape
    half = (cols, rows // 2)
    return call(
        final_kernel,
        none,
        [part, received],
        [like(*half, dtype=f32)] * 2,
        [pltpu.VMEM(half, f32), pltpu.VMEM(half, f32), pltpu.SemaphoreType.DMA((2,))],
        far=(2, 3),
    )


def local(
    inputs,
    key_grad,
    value_grad,
    key_weight,
    value_weight,
    global_params,
    momentum,
    local_params,
    fragment,
    step,
    outer_rates,
):
    iy, iz, ic, ix = (lax.axis_index(a).astype(jnp.int32) for a in ("y", "z", "c", "x"))
    none = jnp.zeros((1,), jnp.int32)
    tokens_in = inputs[0]
    local_now = local_params[0]
    base = jnp.stack([
        ((iy + d) % 4) * 4 + z * 2
        for d, z in ((2, 1 - iz), (1, iz), (2, iz), (3, 1 - iz), (1, 1 - iz), (3, iz), (0, 1 - iz), (0, iz))
    ])

    weight = join(none, key_weight[0], value_weight[0])
    weight, key_part, value_part = fence((weight, key_grad[0], value_grad[0]))
    w1, w3, w2 = shift(weight, "y", -1), shift(weight, "y", -3), shift(weight, "y", 2)
    grads, pack = prepare(base + 1 - ic, tokens_in, key_part, value_part)
    pack = shift(pack, "c", 1)
    sent = local_now.astype(bf16)
    pair_sib = lax.ppermute(sent, "r", [(k, k ^ 1) for k in range(4)])

    pack, grads_b = fence((pack, grads))
    going_up, going_down, relayed, own, sib = partials(base + ic, tokens_in, grads, pack)
    h1 = shift(grads_b, "x", 1)
    pair = (sent.astype(f32) + pair_sib.astype(f32)).astype(bf16)
    pair_sib = lax.ppermute(pair, "r", [(k, k ^ 3) for k in range(4)])

    w1, w2, w3, h1, going_up, going_down = fence((w1, w2, w3, h1, going_up, going_down))
    near0, pick1, pick2, pick3 = pick(((ix - iy) % 4).reshape(1), [weight, w1, w2, w3])
    near1, near3 = shift(pick1, "x", 1), shift(pick3, "x", 3)
    over0 = shift(near0, "z", 1)
    up, down = shift(going_up, "y", 1), shift(going_down, "y", 3)

    near1, near3, over0, pick2, pair_sib = fence((near1, near3, over0, pick2, pair_sib))
    near2 = shift(pick2, "x", 2)
    over1, over3 = shift(near1, "z", 1), shift(near3, "z", 1)

    near2, up, down, over1, grads_f = fence((near2, up, down, over1, grads))
    up_o, down_m = call(relay_kernel, none, [relayed, up, down], [like(*up.shape[1:])] * 2)
    up_o, down_m = shift(up_o, "y", 1), shift(down_m, "y", 3)
    over2 = shift(near2, "z", 1)
    h3, h2 = shift(grads_f, "x", 3), shift(grads_f, "x", 2)
    own_heads, sib_heads = [grads, h1], [sib, shift(h1, "c", 1)]
    near_own, near_sib = early_slots(none, own_heads, sib_heads, [near0, near1])
    over_own, over_sib = early_slots(none, own_heads, sib_heads, [over0, over1])
    up_o, down_m, near_own, near_sib, over_own, over_sib = fence((up_o, down_m, near_own, near_sib, over_own, over_sib))
    other = call(other_kernel, none, [own, up_o, down], [like(*own.shape[1:])])[0]
    received = shift(other, "z", 1)

    h3, h2, over3, over2, other = fence((h3, h2, over3, over2, other))
    heads, near, over = [h3, h2], [near3, near2], [over3, over2]
    loose = loose_blocks(none, [shift(h, "c", 1) for h in heads], near, over, [near_sib, over_sib])
    loose = shift(loose, "c", 1)
    back = back_blocks(jnp.stack([iz * 2 + ic, (1 - iz) * 2 + ic]), heads, near, over, [near_own, over_own])
    mine = call(mine_kernel, none, [own, up, down_m], [like(own.shape[2], own.shape[1], dtype=f32)])[0]
    back = place(jnp.stack([iz * 2 + 1 - ic, (1 - iz) * 2 + 1 - ic]), loose, back)
    back, mine, received = fence((back, mine, received))
    wgrad_k, wgrad_v = final_sum(none, mine, received)

    total = pair.astype(f32) + pair_sib.astype(f32)
    count_frag = outer_rates.shape[0]
    chosen = (jnp.arange(count_frag, dtype=jnp.int32) == fragment[0]).astype(f32)
    warm = jnp.minimum(1.0, (step[0].astype(f32) + 1.0) / WARMUP)
    rate = jnp.sum(chosen * outer_rates) * warm
    replicas = lax.axis_size("r")
    fresh_global, fresh_momentum = outer_step(global_params, momentum, total / replicas, rate)
    fresh_local = mixing * local_now + (1.0 - mixing) * fresh_global
    return (
        back[None],
        wgrad_k[None],
        wgrad_v[None],
        fresh_global,
        fresh_momentum,
        fresh_local[None],
    )


def solution(mesh):
    fine = Mesh(mesh.devices.reshape(4, 4, 2, 2, 4), ("r", "y", "z", "c", "x"))
    fsdp = ("y", "z", "c")
    split = P("r", fsdp, "x")
    in_specs = (
        P("r", fsdp, None),
        split,
        split,
        split,
        split,
        P(fsdp, "x"),
        P(fsdp, "x"),
        split,
        P(),
        P(),
        P(),
    )
    out_specs = (split, split, split, P(fsdp, "x"), P(fsdp, "x"), split)
    return jax.shard_map(local, mesh=fine, in_specs=in_specs, out_specs=out_specs, check_vma=False)
```

time: 144 us -> 124 us (0.86)
  the two profiles are of different devices: /device:TPU:64 before, /device:TPU:6 now
where the time goes in v2:
time: 124 us
  waiting for transfers between devices  42.2 us (34%)
  starting transfers between devices  35.4 us (29%)
  Pallas kernels  34.5 us (28%)
  local copies, waits for them, and re-layouts  4.99 us (4%)
  other arithmetic  3.69 us (3%)
  between operations  3.15 us (3%)
    ppermute x23, waiting for transfers between devices, shift(): return lax.ppermute(a, axis, [(i, (i + by) % n) for i in range(n)])  36.7 us
    pallas_call x13, Pallas kernels, call(): pl.pallas_call(kernel, out_shape=[space(a.shape, a.dtype) for a, space in...  34.5 us
    ppermute x23, starting transfers between devices, shift(): return lax.ppermute(a, axis, [(i, (i + by) % n) for i in range(n)])  28.3 us
    ppermute x1, waiting for transfers between devices, local(): pair_sib = lax.ppermute(sent, 'r', [(k, k ^ 1) for k in range(4)])  5.53 us
    unnamed x42, local copies, waits for them, and re-layouts  4.91 us
    ppermute x1, starting transfers between devices, local(): pair_sib = lax.ppermute(pair, 'r', [(k, k ^ 3) for k in range(4)])  3.83 us
    ppermute x1, starting transfers between devices, local(): pair_sib = lax.ppermute(sent, 'r', [(k, k ^ 1) for k in range(4)])  3.36 us
    broadcast_in_dim x1, other arithmetic, local(): fresh_local[None]  2.86 us
  transfers between devices with their start and end apart: 25, of which 12 were waited for; matrix products, arithmetic and copies ran while one was open for 3% of the time, Pallas kernels for 18%

profile of v2, /device:TPU:6, one launch (start us, length us, event | category | flops | bytes accessed | tf_op | source)
XLA Modules:
  0.0 124.0 jit_solution(5525556799543026542)
XLA Ops:
  1.9 5.3 %shard_map.155 = (bf16[512,512]{1,0:T(8,128)(2,1)}, bf16[9,512,512]{2,1,0:T(8,128)(2,1)}) custom-call(s32[8]{0:T(128)S(1)} %get-tuple-element.116.where, bf16[512,8192]{1,0:T(8,128)(2,1)} %bitcast.35, bf16[512,256]{1,0:T(8,128)(2,1)} %bitcast.38, bf16[512,256]{1,0:T(8,128)(2,1)} %bitcast.39), custom_call_target="tpu_custom_call" | custom-call | tf_op jit(solution)/shard_map/pallas_call | solution.py:41
  7.3 3.4 %collective-permute-start.8 = (bf16[64,2048]{1,0:T(8,128)(2,1)S(1)}, bf16[64,2048]{1,0:T(8,128)(2,1)S(1)}, u32[]{:S(2)}, u32[]{:S(2)}) collective-permute-start(bf16[64,2048]{1,0:T(8,128)(2,1)S(1)} %bitcast_convert_fusion), channel_id=1, source_target_pairs={{0,64},{64,0},{128,192},{192,128},{1,65},{65,1},{129,193},{193,129... | collective-permute-start | bytes 786440 | tf_op jit(solution)/shard_map/ppermute | solution.py:302
  10.7 3.0 %collective-permute-start = (bf16[512,512]{1,0:T(8,128)(2,1)S(1)}, bf16[512,512]{1,0:T(8,128)(2,1)S(1)}, u32[]{:S(2)}, u32[]{:S(2)}) collective-permute-start(bf16[512,512]{1,0:T(8,128)(2,1)S(1)} %shard_map.154.refs_0_), channel_id=1, source_target_pairs={{0,48},{16,0},{32,16},{48,32},{1,49},{17,1},{33,17},{49,33},{2,50}... | collective-permute-start | bytes 1572872 | tf_op jit(solution)/shard_map/ppermute | solution.py:20
  15.5 2.2 %collective-permute-start.4 = (bf16[512,512]{1,0:T(8,128)(2,1)}, bf16[512,512]{1,0:T(8,128)(2,1)S(1)}, u32[]{:S(2)}, u32[]{:S(2)}) collective-permute-start(bf16[512,512]{1,0:T(8,128)(2,1)} %get-tuple-element.79.grads.refs_0_), channel_id=1, source_target_pairs={{0,1},{1,2},{2,3},{3,0},{4,5},{5,6},{6,7},{7,4},{8,9},{9,10},{10,1... | collective-permute-start | bytes 1572872 | tf_op jit(solution)/shard_map/ppermute | solution.py:20
  17.7 5.5 %collective-permute-done.8 = bf16[64,2048]{1,0:T(8,128)(2,1)S(1)} collective-permute-done((bf16[64,2048]{1,0:T(8,128)(2,1)S(1)}, bf16[64,2048]{1,0:T(8,128)(2,1)S(1)}, u32[]{:S(2)}, u32[]{:S(2)}) %collective-permute-start.8) | collective-permute-done | bytes 262176 | tf_op jit(solution)/shard_map/ppermute | solution.py:302
  23.3 3.8 %collective-permute-start.9 = (bf16[64,2048]{1,0:T(8,128)(2,1)S(1)}, bf16[64,2048]{1,0:T(8,128)(2,1)}, u32[]{:S(2)}, u32[]{:S(2)}) collective-permute-start(bf16[64,2048]{1,0:T(8,128)(2,1)S(1)} %add_convert_fusion), channel_id=1, source_target_pairs={{0,192},{64,128},{128,64},{192,0},{1,193},{65,129},{129,65},{193,1... | collective-permute-start | bytes 786440 | tf_op jit(solution)/shard_map/ppermute | solution.py:308
  27.1 9.5 %shard_map.156 = (bf16[2,512,512]{2,1,0:T(8,128)(2,1)S(1)}, bf16[2,512,512]{2,1,0:T(8,128)(2,1)S(1)}, bf16[2,512,512]{2,1,0:T(8,128)(2,1)S(1)}, bf16[2,512,512]{2,1,0:T(8,128)(2,1)S(1)}, bf16[512,512]{1,0:T(8,128)(2,1)S(1)}) custom-call(s32[8]{0:T(128)S(1)} %get-tuple-element.115.where, bf16[512,8192]{1,0:T(8,128)(2,1)} %bitcast.36, ...), custom_call_target="tpu_custom_call" | custom-call | flops 4294967296 | tf_op jit(solution)/shard_map/pallas_call | solution.py:41
  36.7 3.5 %collective-permute-done.2.refs_3_ = bf16[512,512]{1,0:T(8,128)(2,1)S(1)} collective-permute-done((bf16[512,512]{1,0:T(8,128)(2,1)S(1)}, bf16[512,512]{1,0:T(8,128)(2,1)S(1)}, u32[]{:S(2)}, u32[]{:S(2)}) %collective-permute-start.2) | collective-permute-done | bytes 524320 | tf_op jit(solution)/shard_map/ppermute | solution.py:20
  42.6 1.9 %collective-permute-start.7 = (bf16[512,512]{1,0:T(8,128)(2,1)S(1)}, bf16[512,512]{1,0:T(8,128)(2,1)S(1)}, u32[]{:S(2)}, u32[]{:S(2)}) collective-permute-start(bf16[512,512]{1,0:T(8,128)(2,1)S(1)} %get-tuple-element.73.refs_4_), channel_id=1, source_target_pairs={{0,8},{8,0},{1,9},{9,1},{2,10},{10,2},{3,11},{11,3},{4,12},{12,4},... | collective-permute-start | bytes 1572872 | tf_op jit(solution)/shard_map/ppermute | solution.py:20
  44.5 3.2 %collective-permute-start.12 = (bf16[2,512,512]{2,1,0:T(8,128)(2,1)S(1)}, bf16[2,512,512]{2,1,0:T(8,128)(2,1)S(1)}, u32[]{:S(2)}, u32[]{:S(2)}) collective-permute-start(bf16[2,512,512]{2,1,0:T(8,128)(2,1)S(1)} %get-tuple-element.77), channel_id=1, source_target_pairs={{0,48},{16,0},{32,16},{48,32},{1,49},{17,1},{33,17},{49,33},{2,50}... | collective-permute-start | bytes 3145736 | tf_op jit(solution)/shard_map/ppermute | solution.py:20
  47.8 6.7 %collective-permute-done.5.refs_5_ = bf16[512,512]{1,0:T(8,128)(2,1)S(1)} collective-permute-done((bf16[512,512]{1,0:T(8,128)(2,1)S(1)}, bf16[512,512]{1,0:T(8,128)(2,1)S(1)}, u32[]{:S(2)}, u32[]{:S(2)}) %collective-permute-start.5) | collective-permute-done | bytes 524320 | tf_op jit(solution)/shard_map/ppermute | solution.py:20
  59.2 10.9 %collective-permute-done.10.refs_3_ = bf16[512,512]{1,0:T(8,128)(2,1)S(1)} collective-permute-done((bf16[512,512]{1,0:T(8,128)(2,1)S(1)}, bf16[512,512]{1,0:T(8,128)(2,1)S(1)}, u32[]{:S(2)}, u32[]{:S(2)}) %collective-permute-start.10) | collective-permute-done | bytes 524320 | tf_op jit(solution)/shard_map/ppermute | solution.py:20
  70.5 3.2 %collective-permute-start.19 = (bf16[512,512]{1,0:T(8,128)(2,1)S(1)}, bf16[512,512]{1,0:T(8,128)(2,1)S(1)}, u32[]{:S(2)}, u32[]{:S(2)}) collective-permute-start(bf16[512,512]{1,0:T(8,128)(2,1)S(1)} %get-tuple-element.87), channel_id=1, source_target_pairs={{0,48},{16,0},{32,16},{48,32},{1,49},{17,1},{33,17},{49,33},{2,50}... | collective-permute-start | bytes 1572872 | tf_op jit(solution)/shard_map/ppermute | solution.py:20
  76.1 2.3 %collective-permute-start.15 = (bf16[512,512]{1,0:T(8,128)(2,1)}, bf16[512,512]{1,0:T(8,128)(2,1)S(1)}, u32[]{:S(2)}, u32[]{:S(2)}) collective-permute-start(bf16[512,512]{1,0:T(8,128)(2,1)} %get-tuple-element.79.grads.refs_0_), channel_id=1, source_target_pairs={{0,2},{1,3},{2,0},{3,1},{4,6},{5,7},{6,4},{7,5},{8,10},{9,11},{10,... | collective-permute-start | bytes 1572872 | tf_op jit(solution)/shard_map/ppermute | solution.py:20
  78.5 5.1 %collective-permute-done.18.up = bf16[512,512]{1,0:T(8,128)(2,1)S(1)} collective-permute-done((bf16[512,512]{1,0:T(8,128)(2,1)S(1)}, bf16[512,512]{1,0:T(8,128)(2,1)S(1)}, u32[]{:S(2)}, u32[]{:S(2)}) %collective-permute-start.18) | collective-permute-done | bytes 524320 | tf_op jit(solution)/shard_map/ppermute | solution.py:20
  85.4 2.9 %shard_map.159 = (f32[512,512]{1,0:T(8,128)S(1)}, f32[512,512]{1,0:T(8,128)S(1)}) custom-call(s32[1]{0:T(128)} %constant.68.clone.1._, bf16[512,512]{1,0:T(8,128)(2,1)} %get-tuple-element.79.grads.refs_0_, bf16[512,512]{1,0:T(8,128)(2,1)} %copy-done.16, bf16[512,512]{1,0:T(8,128)(2,1)} %copy-done.12, bf16[512,512]{1,0:T(8,128)(2,1)S(1)} %collective-permute-done.20.refs_3_, ...), custom_call_target="tpu_custom_call" | custom-call | flops 1073741824 | tf_op jit(solution)/shard_map/pallas_call | solution.py:41
  90.3 2.9 %shard_map.160 = (f32[512,512]{1,0:T(8,128)S(1)}, f32[512,512]{1,0:T(8,128)S(1)}) custom-call(s32[1]{0:T(128)} %constant.68.clone.1._, bf16[512,512]{1,0:T(8,128)(2,1)} %get-tuple-element.79.grads.refs_0_, bf16[512,512]{1,0:T(8,128)(2,1)} %copy-done.16, bf16[512,512]{1,0:T(8,128)(2,1)} %copy-done.12, bf16[512,512]{1,0:T(8,128)(2,1)S(1)} %collective-permute-done.20.refs_3_, ...), custom_call_target="tpu_custom_call" | custom-call | flops 1073741824 | tf_op jit(solution)/shard_map/pallas_call | solution.py:41
  95.3 3.9 %collective-permute-done.14.refs_0_ = bf16[512,512]{1,0:T(8,128)(2,1)S(1)} collective-permute-done((bf16[512,512]{1,0:T(8,128)(2,1)}, bf16[512,512]{1,0:T(8,128)(2,1)S(1)}, u32[]{:S(2)}, u32[]{:S(2)}) %collective-permute-start.14) | collective-permute-done | bytes 524320 | tf_op jit(solution)/shard_map/ppermute | solution.py:20
  102.0 3.6 %shard_map.162 = bf16[2,512,512]{2,1,0:T(8,128)(2,1)} custom-call(s32[1]{0:T(128)} %constant.68.clone.1._, bf16[512,512]{1,0:T(8,128)(2,1)S(1)} %collective-permute-done.21.refs_0_, bf16[512,512]{1,0:T(8,128)(2,1)S(1)} %collective-permute-done.22.refs_1_, bf16[512,512]{1,0:T(8,128)(2,1)} %copy-done.14, bf16[512,512]{1,0:T(8,128)(2,1)S(1)} %collective-permute-done.10.refs_3_, ...), custom_call_target="tpu_custom_call" | custom-call | tf_op jit(solution)/shard_map/pallas_call | solution.py:41
  108.8 2.9 %fusion.1 = (f32[1,64,2048]{2,1,0:T(8,128)}, f32[64,2048]{1,0:T(8,128)}, f32[64,2048]{1,0:T(8,128)}) fusion(f32[1,64,2048]{2,1,0:T(8,128)} %param.18, f32[64,2048]{1,0:T(8,128)} %param.16, bf16[64,2048]{1,0:T(8,128)(2,1)} %collective-permute-done.9, bf16[64,2048]{1,0:T(8,128)(2,1)S(1)} %add_convert_fusion, f32[]{:T(128)S(6)} %mul.61, f32[64,2048]{1,0:T(8,128)} %param.17), kind=kLoop, calls=%fused_computation.3 | loop fusion | flops 1703936 | bytes 3670020 | tf_op jit(solution)/shard_map/broadcast_in_dim | solution.py:356
  113.1 3.9 %shard_map.163._ = bf16[512,2048]{1,0:T(8,128)(2,1)} custom-call(s32[2]{0:T(128)S(1)} %pad_add_fusion.1.where, bf16[512,512]{1,0:T(8,128)(2,1)S(1)} %copy-done.8, bf16[512,512]{1,0:T(8,128)(2,1)S(1)} %copy-done.10, bf16[512,512]{1,0:T(8,128)(2,1)} %copy-done.14, bf16[512,512]{1,0:T(8,128)(2,1)S(1)} %collective-permute-done.10.refs_3_, ...), custom_call_target="tpu_custom_call" | custom-call | tf_op jit(solution)/shard_map/pallas_call | solution.py:41
  117.0 2.2 %shard_map.164 = bf16[512,2048]{1,0:T(8,128)(2,1)} custom-call(s32[2]{0:T(128)S(1)} %pad_add_fusion.where, bf16[2,512,512]{2,1,0:T(8,128)(2,1)} %collective-permute-done.23.blocks, bf16[512,2048]{1,0:T(8,128)(2,1)} %shard_map.163._), custom_call_target="tpu_custom_call", output_to_operand_aliasing={{}: (2, {})} | custom-call | tf_op jit(solution)/shard_map/pallas_call | solution.py:41
  119.2 2.5 %collective-permute-done.24.received = bf16[512,512]{1,0:T(8,128)(2,1)} collective-permute-done((bf16[512,512]{1,0:T(8,128)(2,1)}, bf16[512,512]{1,0:T(8,128)(2,1)}, u32[]{:S(2)}, u32[]{:S(2)}) %collective-permute-start.24) | collective-permute-done | bytes 524320 | tf_op jit(solution)/shard_map/ppermute | solution.py:20
  121.7 2.2 %shard_map.166 = (f32[512,256]{1,0:T(8,128)}, f32[512,256]{1,0:T(8,128)}) custom-call(s32[1]{0:T(128)} %constant.68.clone.1._, f32[512,512]{1,0:T(8,128)S(1)} %shard_map.165.part, bf16[512,512]{1,0:T(8,128)(2,1)} %collective-permute-done.24.received), custom_call_target="tpu_custom_call" | custom-call | tf_op jit(solution)/shard_map/pallas_call | solution.py:41
  (89 shorter events, 24.3 us)
Async XLA Ops:
  7.2 8.3 %collective-permute-start.3 = (bf16[9,512,512]{2,1,0:T(8,128)(2,1)}, bf16[9,512,512]{2,1,0:T(8,128)(2,1)}, u32[]{:S(2)}, u32[]{:S(2)}) collective-permute-start(bf16[9,512,512]{2,1,0:T(8,128)(2,1)} %get-tuple-element.62), channel_id=1, source_target_pairs={{0,4},{4,0},{1,5},{5,1},{2,6},{6,2},{3,7},{7,3},{8,12},{12,8},{9,1... | collective-permute-start | bytes 14155784 | tf_op jit(solution)/shard_map/ppermute | solution.py:20
  7.3 15.9 %collective-permute-start.8 = (bf16[64,2048]{1,0:T(8,128)(2,1)S(1)}, bf16[64,2048]{1,0:T(8,128)(2,1)S(1)}, u32[]{:S(2)}, u32[]{:S(2)}) collective-permute-start(bf16[64,2048]{1,0:T(8,128)(2,1)S(1)} %bitcast_convert_fusion), channel_id=1, source_target_pairs={{0,64},{64,0},{128,192},{192,128},{1,65},{65,1},{129,193},{193,129... | collective-permute-start | bytes 786440 | tf_op jit(solution)/shard_map/ppermute | solution.py:302
  10.7 26.0 %collective-permute-start = (bf16[512,512]{1,0:T(8,128)(2,1)S(1)}, bf16[512,512]{1,0:T(8,128)(2,1)S(1)}, u32[]{:S(2)}, u32[]{:S(2)}) collective-permute-start(bf16[512,512]{1,0:T(8,128)(2,1)S(1)} %shard_map.154.refs_0_), channel_id=1, source_target_pairs={{0,48},{16,0},{32,16},{48,32},{1,49},{17,1},{33,17},{49,33},{2,50}... | collective-permute-start | bytes 1572872 | tf_op jit(solution)/shard_map/ppermute | solution.py:20
  13.7 23.0 %collective-permute-start.1 = (bf16[512,512]{1,0:T(8,128)(2,1)S(1)}, bf16[512,512]{1,0:T(8,128)(2,1)S(1)}, u32[]{:S(2)}, u32[]{:S(2)}) collective-permute-start(bf16[512,512]{1,0:T(8,128)(2,1)S(1)} %shard_map.154.refs_0_), channel_id=1, source_target_pairs={{0,32},{16,48},{32,0},{48,16},{1,33},{17,49},{33,1},{49,17},{2,34}... | collective-permute-start | bytes 1572872 | tf_op jit(solution)/shard_map/ppermute | solution.py:20
  14.3 25.9 %collective-permute-start.2 = (bf16[512,512]{1,0:T(8,128)(2,1)S(1)}, bf16[512,512]{1,0:T(8,128)(2,1)S(1)}, u32[]{:S(2)}, u32[]{:S(2)}) collective-permute-start(bf16[512,512]{1,0:T(8,128)(2,1)S(1)} %shard_map.154.refs_0_), channel_id=1, source_target_pairs={{0,16},{16,32},{32,48},{48,0},{1,17},{17,33},{33,49},{49,1},{2,18}... | collective-permute-start | bytes 1572872 | tf_op jit(solution)/shard_map/ppermute | solution.py:20
  15.5 24.7 %collective-permute-start.4 = (bf16[512,512]{1,0:T(8,128)(2,1)}, bf16[512,512]{1,0:T(8,128)(2,1)S(1)}, u32[]{:S(2)}, u32[]{:S(2)}) collective-permute-start(bf16[512,512]{1,0:T(8,128)(2,1)} %get-tuple-element.79.grads.refs_0_), channel_id=1, source_target_pairs={{0,1},{1,2},{2,3},{3,0},{4,5},{5,6},{6,7},{7,4},{8,9},{9,10},{10,1... | collective-permute-start | bytes 1572872 | tf_op jit(solution)/shard_map/ppermute | solution.py:20
  23.3 21.2 %collective-permute-start.9 = (bf16[64,2048]{1,0:T(8,128)(2,1)S(1)}, bf16[64,2048]{1,0:T(8,128)(2,1)}, u32[]{:S(2)}, u32[]{:S(2)}) collective-permute-start(bf16[64,2048]{1,0:T(8,128)(2,1)S(1)} %add_convert_fusion), channel_id=1, source_target_pairs={{0,192},{64,128},{128,64},{192,0},{1,193},{65,129},{129,65},{193,1... | collective-permute-start | bytes 786440 | tf_op jit(solution)/shard_map/ppermute | solution.py:308
  40.5 13.9 %collective-permute-start.5 = (bf16[512,512]{1,0:T(8,128)(2,1)S(1)}, bf16[512,512]{1,0:T(8,128)(2,1)S(1)}, u32[]{:S(2)}, u32[]{:S(2)}) collective-permute-start(bf16[512,512]{1,0:T(8,128)(2,1)S(1)} %get-tuple-element.71), channel_id=1, source_target_pairs={{0,1},{1,2},{2,3},{3,0},{4,5},{5,6},{6,7},{7,4},{8,9},{9,10},{10,1... | collective-permute-start | bytes 1572872 | tf_op jit(solution)/shard_map/ppermute | solution.py:20
  41.1 14.8 %collective-permute-start.6 = (bf16[512,512]{1,0:T(8,128)(2,1)S(1)}, bf16[512,512]{1,0:T(8,128)(2,1)S(1)}, u32[]{:S(2)}, u32[]{:S(2)}) collective-permute-start(bf16[512,512]{1,0:T(8,128)(2,1)S(1)} %get-tuple-element.72), channel_id=1, source_target_pairs={{0,3},{1,0},{2,1},{3,2},{4,7},{5,4},{6,5},{7,6},{8,11},{9,8},{10,9... | collective-permute-start | bytes 1572872 | tf_op jit(solution)/shard_map/ppermute | solution.py:20
  42.6 13.5 %collective-permute-start.7 = (bf16[512,512]{1,0:T(8,128)(2,1)S(1)}, bf16[512,512]{1,0:T(8,128)(2,1)S(1)}, u32[]{:S(2)}, u32[]{:S(2)}) collective-permute-start(bf16[512,512]{1,0:T(8,128)(2,1)S(1)} %get-tuple-element.73.refs_4_), channel_id=1, source_target_pairs={{0,8},{8,0},{1,9},{9,1},{2,10},{10,2},{3,11},{11,3},{4,12},{12,4},... | collective-permute-start | bytes 1572872 | tf_op jit(solution)/shard_map/ppermute | solution.py:20
  44.5 25.6 %collective-permute-start.11 = (bf16[2,512,512]{2,1,0:T(8,128)(2,1)S(1)}, bf16[2,512,512]{2,1,0:T(8,128)(2,1)S(1)}, u32[]{:S(2)}, u32[]{:S(2)}) collective-permute-start(bf16[2,512,512]{2,1,0:T(8,128)(2,1)S(1)} %get-tuple-element.76), channel_id=1, source_target_pairs={{0,16},{16,32},{32,48},{48,0},{1,17},{17,33},{33,49},{49,1},{2,18}... | collective-permute-start | bytes 3145736 | tf_op jit(solution)/shard_map/ppermute | solution.py:20
  44.5 25.6 %collective-permute-start.12 = (bf16[2,512,512]{2,1,0:T(8,128)(2,1)S(1)}, bf16[2,512,512]{2,1,0:T(8,128)(2,1)S(1)}, u32[]{:S(2)}, u32[]{:S(2)}) collective-permute-start(bf16[2,512,512]{2,1,0:T(8,128)(2,1)S(1)} %get-tuple-element.77), channel_id=1, source_target_pairs={{0,48},{16,0},{32,16},{48,32},{1,49},{17,1},{33,17},{49,33},{2,50}... | collective-permute-start | bytes 3145736 | tf_op jit(solution)/shard_map/ppermute | solution.py:20
  56.1 14.1 %collective-permute-start.10 = (bf16[512,512]{1,0:T(8,128)(2,1)S(1)}, bf16[512,512]{1,0:T(8,128)(2,1)S(1)}, u32[]{:S(2)}, u32[]{:S(2)}) collective-permute-start(bf16[512,512]{1,0:T(8,128)(2,1)S(1)} %get-tuple-element.75), channel_id=1, source_target_pairs={{0,2},{1,3},{2,0},{3,1},{4,6},{5,7},{6,4},{7,5},{8,10},{9,11},{10,... | collective-permute-start | bytes 1572872 | tf_op jit(solution)/shard_map/ppermute | solution.py:20
  57.5 12.6 %collective-permute-start.13 = (bf16[512,512]{1,0:T(8,128)(2,1)S(1)}, bf16[512,512]{1,0:T(8,128)(2,1)S(1)}, u32[]{:S(2)}, u32[]{:S(2)}) collective-permute-start(bf16[512,512]{1,0:T(8,128)(2,1)S(1)} %collective-permute-done.5.refs_5_), channel_id=1, source_target_pairs={{0,8},{8,0},{1,9},{9,1},{2,10},{10,2},{3,11},{11,3},{4,12},{12,4},... | collective-permute-start | bytes 1572872 | tf_op jit(solution)/shard_map/ppermute | solution.py:20
  59.2 16.9 %collective-permute-start.20 = (bf16[512,512]{1,0:T(8,128)(2,1)S(1)}, bf16[512,512]{1,0:T(8,128)(2,1)S(1)}, u32[]{:S(2)}, u32[]{:S(2)}) collective-permute-start(bf16[512,512]{1,0:T(8,128)(2,1)S(1)} %collective-permute-done.4.refs_1_), channel_id=1, source_target_pairs={{0,4},{4,0},{1,5},{5,1},{2,6},{6,2},{3,7},{7,3},{8,12},{12,8},{9,1... | collective-permute-start | bytes 1572872 | tf_op jit(solution)/shard_map/ppermute | solution.py:20
  70.4 13.2 %collective-permute-start.18 = (bf16[512,512]{1,0:T(8,128)(2,1)S(1)}, bf16[512,512]{1,0:T(8,128)(2,1)S(1)}, u32[]{:S(2)}, u32[]{:S(2)}) collective-permute-start(bf16[512,512]{1,0:T(8,128)(2,1)S(1)} %get-tuple-element.86), channel_id=1, source_target_pairs={{0,16},{16,32},{32,48},{48,0},{1,17},{17,33},{33,49},{49,1},{2,18}... | collective-permute-start | bytes 1572872 | tf_op jit(solution)/shard_map/ppermute | solution.py:20
  70.5 23.7 %collective-permute-start.19 = (bf16[512,512]{1,0:T(8,128)(2,1)S(1)}, bf16[512,512]{1,0:T(8,128)(2,1)S(1)}, u32[]{:S(2)}, u32[]{:S(2)}) collective-permute-start(bf16[512,512]{1,0:T(8,128)(2,1)S(1)} %get-tuple-element.87), channel_id=1, source_target_pairs={{0,48},{16,0},{32,16},{48,32},{1,49},{17,1},{33,17},{49,33},{2,50}... | collective-permute-start | bytes 1572872 | tf_op jit(solution)/shard_map/ppermute | solution.py:20
  73.7 21.5 %collective-permute-start.16 = (bf16[512,512]{1,0:T(8,128)(2,1)S(1)}, bf16[512,512]{1,0:T(8,128)(2,1)S(1)}, u32[]{:S(2)}, u32[]{:S(2)}) collective-permute-start(bf16[512,512]{1,0:T(8,128)(2,1)S(1)} %collective-permute-done.6.refs_2_), channel_id=1, source_target_pairs={{0,8},{8,0},{1,9},{9,1},{2,10},{10,2},{3,11},{11,3},{4,12},{12,4},... | collective-permute-start | bytes 1572872 | tf_op jit(solution)/shard_map/ppermute | solution.py:20
  75.6 23.6 %collective-permute-start.14 = (bf16[512,512]{1,0:T(8,128)(2,1)}, bf16[512,512]{1,0:T(8,128)(2,1)S(1)}, u32[]{:S(2)}, u32[]{:S(2)}) collective-permute-start(bf16[512,512]{1,0:T(8,128)(2,1)} %get-tuple-element.79.grads.refs_0_), channel_id=1, source_target_pairs={{0,3},{1,0},{2,1},{3,2},{4,7},{5,4},{6,5},{7,6},{8,11},{9,8},{10,9... | collective-permute-start | bytes 1572872 | tf_op jit(solution)/shard_map/ppermute | solution.py:20
  76.1 23.1 %collective-permute-start.15 = (bf16[512,512]{1,0:T(8,128)(2,1)}, bf16[512,512]{1,0:T(8,128)(2,1)S(1)}, u32[]{:S(2)}, u32[]{:S(2)}) collective-permute-start(bf16[512,512]{1,0:T(8,128)(2,1)} %get-tuple-element.79.grads.refs_0_), channel_id=1, source_target_pairs={{0,2},{1,3},{2,0},{3,1},{4,6},{5,7},{6,4},{7,5},{8,10},{9,11},{10,... | collective-permute-start | bytes 1572872 | tf_op jit(solution)/shard_map/ppermute | solution.py:20
  83.6 15.6 %collective-permute-start.17 = (bf16[512,512]{1,0:T(8,128)(2,1)S(1)}, bf16[512,512]{1,0:T(8,128)(2,1)S(1)}, u32[]{:S(2)}, u32[]{:S(2)}) collective-permute-start(bf16[512,512]{1,0:T(8,128)(2,1)S(1)} %collective-permute-done.10.refs_3_), channel_id=1, source_target_pairs={{0,8},{8,0},{1,9},{9,1},{2,10},{10,2},{3,11},{11,3},{4,12},{12,4},... | collective-permute-start | bytes 1572872 | tf_op jit(solution)/shard_map/ppermute | solution.py:20
  99.3 2.6 %collective-permute-start.22 = (bf16[512,512]{1,0:T(8,128)(2,1)S(1)}, bf16[512,512]{1,0:T(8,128)(2,1)S(1)}, u32[]{:S(2)}, u32[]{:S(2)}) collective-permute-start(bf16[512,512]{1,0:T(8,128)(2,1)S(1)} %collective-permute-done.15.refs_1_), channel_id=1, source_target_pairs={{0,4},{4,0},{1,5},{5,1},{2,6},{6,2},{3,7},{7,3},{8,12},{12,8},{9,1... | collective-permute-start | bytes 1572872 | tf_op jit(solution)/shard_map/ppermute | solution.py:20
  105.6 11.4 %collective-permute-start.23 = (bf16[2,512,512]{2,1,0:T(8,128)(2,1)}, bf16[2,512,512]{2,1,0:T(8,128)(2,1)}, u32[]{:S(2)}, u32[]{:S(2)}) collective-permute-start(bf16[2,512,512]{2,1,0:T(8,128)(2,1)} %shard_map.162), channel_id=1, source_target_pairs={{0,4},{4,0},{1,5},{5,1},{2,6},{6,2},{3,7},{7,3},{8,12},{12,8},{9,1... | collective-permute-start | bytes 3145736 | tf_op jit(solution)/shard_map/ppermute | solution.py:20
  107.2 14.5 %collective-permute-start.24 = (bf16[512,512]{1,0:T(8,128)(2,1)}, bf16[512,512]{1,0:T(8,128)(2,1)}, u32[]{:S(2)}, u32[]{:S(2)}) collective-permute-start(bf16[512,512]{1,0:T(8,128)(2,1)} %copy-done.6), channel_id=1, source_target_pairs={{0,8},{8,0},{1,9},{9,1},{2,10},{10,2},{3,11},{11,3},{4,12},{12,4},... | collective-permute-start | bytes 1572872 | tf_op jit(solution)/shard_map/ppermute | solution.py:20
  (22 other events, 324.8 us)

commit v3 on v2

--- a/solution.py
+++ b/solution.py
@@ -190,17 +190,15 @@
 
 
 def loose_kernel(_, *refs):
-    out = refs[8]
-
     def emit(k, block):
-        out[k] = block
-
-    late_slots(refs[:6], refs[6:8], *refs[9:], emit)
+        refs[8 + k][...] = block
+
+    late_slots(refs[:6], refs[6:8], *refs[10:], emit)
 
 
 def loose_blocks(none, heads, near, over, accs):
     ins = [*heads, *near, *over, *accs]
-    return call(loose_kernel, none, ins, [like(2, *accs[0].shape)], late_scratch(accs[0]), far=(2, 4, 6, 7))[0]
+    return call(loose_kernel, none, ins, [like(*accs[0].shape)] * 2, late_scratch(accs[0]), far=(2, 4, 6, 7))
 
 
 def back_kernel(where, *refs):
@@ -223,16 +221,22 @@
     return call(back_kernel, where, ins, [like(tokens, 4 * width)], scratch, far=(2, 4, 6, 7, 8))[0]
 
 
-def place_kernel(where, blocks, _, out, sems):
-    width = blocks.shape[2]
-    copies = [started(blocks.at[k], column(out, where[k], width), sems.at[k]) for k in range(2)]
+def place_kernel(where, a, b, _, out, sems):
+    width = a.shape[1]
+    copies = [started(block, column(out, where[k], width), sems.at[k]) for k, block in enumerate((a, b))]
     for copy in copies:
         copy.wait()
 
 
 def place(where, blocks, back):
     return call(
-        place_kernel, where, [blocks, back], [like(*back.shape)], [pltpu.SemaphoreType.DMA((2,))], far=(1, 2), aliases={2: 0}
+        place_kernel,
+        where,
+        [*blocks, back],
+        [like(*back.shape)],
+        [pltpu.SemaphoreType.DMA((2,))],
+        far=(2, 3),
+        aliases={3: 0},
     )[0]
 
 
@@ -331,14 +335,12 @@
 
     h3, h2, over3, over2, other = fence((h3, h2, over3, over2, other))
     heads, near, over = [h3, h2], [near3, near2], [over3, over2]
-    loose = loose_blocks(none, [shift(h, "c", 1) for h in heads], near, over, [near_sib, over_sib])
-    loose = shift(loose, "c", 1)
+    sib_heads = [shift(h, "c", 1) for h in heads]
     back = back_blocks(jnp.stack([iz * 2 + ic, (1 - iz) * 2 + ic]), heads, near, over, [near_own, over_own])
+    sib_heads, near, over, back = fence((sib_heads, near, over, back))
+    loose = loose_blocks(none, sib_heads, near, over, [near_sib, over_sib])
+    loose = [shift(block, "c", 1) for block in loose]
     mine = call(mine_kernel, none, [own, up, down_m], [like(own.shape[2], own.shape[1], dtype=f32)])[0]
-    back = place(jnp.stack([iz * 2 + 1 - ic, (1 - iz) * 2 + 1 - ic]), loose, back)
-    back, mine, received = fence((back, mine, received))
-    wgrad_k, wgrad_v = final_sum(none, mine, received)
-
     total = pair.astype(f32) + pair_sib.astype(f32)
     count_frag = outer_rates.shape[0]
     chosen = (jnp.arange(count_frag, dtype=jnp.int32) == fragment[0]).astype(f32)
@@ -347,6 +349,12 @@
     replicas = lax.axis_size("r")
     fresh_global, fresh_momentum = outer_step(global_params, momentum, total / replicas, rate)
     fresh_local = mixing * local_now + (1.0 - mixing) * fresh_global
+    fresh_global, fresh_momentum, fresh_local, back, loose, mine, received = fence(
+        (fresh_global, fresh_momentum, fresh_local, back, loose, mine, received)
+    )
+    back = place(jnp.stack([iz * 2 + 1 - ic, (1 - iz) * 2 + 1 - ic]), loose, back)
+    wgrad_k, wgrad_v = final_sum(none, mine, received)
+
     return (
         back[None],
         wgrad_k[None],

time: 124 us -> 120 us (0.968)
  waiting for transfers between devices: 42.2 us -> 38.2 us
    ppermute x23 -> x24, waiting for transfers between devices: 36.7 us -> 32.7 us  [shift(): return lax.ppermute(a, axis, [(i, (i + by) % n) for i in range(n)])]
    broadcast_in_dim x1 -> x0, other arithmetic: 2.86 us -> none  [local(): fresh_local[None]]
    add x0 -> x1, other arithmetic: none -> 2.29 us  [local(): fresh_local = mixing * local_now + (1.0 - mixing) * fresh_global]
    unnamed x42 -> x40, local copies, waits for them, and re-layouts: 4.91 us -> 5.38 us
    ppermute x23 -> x24, starting transfers between devices: 28.3 us -> 28.6 us  [shift(): return lax.ppermute(a, axis, [(i, (i + by) % n) for i in range(n)])]
  transfers between devices with their start and end apart: 25 -> 26, of which waited for: 12 -> 10; matrix products, arithmetic and copies ran while one was open for 3% -> 3% of each run, Pallas kernels for 18% -> 21%
where the time goes in v3:
time: 120 us
  waiting for transfers between devices  38.2 us (32%)
  starting transfers between devices  35.8 us (30%)
  Pallas kernels  34 us (28%)
  local copies, waits for them, and re-layouts  5.47 us (5%)
  other arithmetic  3.13 us (3%)
  between operations  3.02 us (3%)
    pallas_call x13, Pallas kernels, call(): pl.pallas_call(kernel, out_shape=[space(a.shape, a.dtype) for a, space in...  34 us
    ppermute x24, waiting for transfers between devices, shift(): return lax.ppermute(a, axis, [(i, (i + by) % n) for i in range(n)])  32.7 us
    ppermute x24, starting transfers between devices, shift(): return lax.ppermute(a, axis, [(i, (i + by) % n) for i in range(n)])  28.6 us
    ppermute x1, waiting for transfers between devices, local(): pair_sib = lax.ppermute(sent, 'r', [(k, k ^ 1) for k in range(4)])  5.53 us
    unnamed x40, local copies, waits for them, and re-layouts  5.38 us
    ppermute x1, starting transfers between devices, local(): pair_sib = lax.ppermute(pair, 'r', [(k, k ^ 3) for k in range(4)])  3.83 us
    ppermute x1, starting transfers between devices, local(): pair_sib = lax.ppermute(sent, 'r', [(k, k ^ 1) for k in range(4)])  3.36 us
  transfers between devices with their start and end apart: 26, of which 10 were waited for; matrix products, arithmetic and copies ran while one was open for 3% of the time, Pallas kernels for 21%

profile of v3, /device:TPU:6, one launch (start us, length us, event | category | flops | bytes accessed | tf_op | source)
XLA Modules:
  0.0 119.6 jit_solution(1032317999900608354)
XLA Ops:
  1.9 5.3 %shard_map.155 = (bf16[512,512]{1,0:T(8,128)(2,1)}, bf16[9,512,512]{2,1,0:T(8,128)(2,1)}) custom-call(s32[8]{0:T(128)S(1)} %get-tuple-element.144.where, bf16[512,8192]{1,0:T(8,128)(2,1)} %bitcast.32, bf16[512,256]{1,0:T(8,128)(2,1)} %bitcast.36, bf16[512,256]{1,0:T(8,128)(2,1)} %bitcast.37), custom_call_target="tpu_custom_call" | custom-call | tf_op jit(solution)/shard_map/pallas_call | solution.py:41
  7.3 3.4 %collective-permute-start = (bf16[64,2048]{1,0:T(8,128)(2,1)S(1)}, bf16[64,2048]{1,0:T(8,128)(2,1)S(1)}, u32[]{:S(2)}, u32[]{:S(2)}) collective-permute-start(bf16[64,2048]{1,0:T(8,128)(2,1)S(1)} %bitcast_convert_fusion), channel_id=1, source_target_pairs={{0,64},{64,0},{128,192},{192,128},{1,65},{65,1},{129,193},{193,129... | collective-permute-start | bytes 786440 | tf_op jit(solution)/shard_map/ppermute | solution.py:306
  10.7 3.0 %collective-permute-start.1 = (bf16[512,512]{1,0:T(8,128)(2,1)S(1)}, bf16[512,512]{1,0:T(8,128)(2,1)S(1)}, u32[]{:S(2)}, u32[]{:S(2)}) collective-permute-start(bf16[512,512]{1,0:T(8,128)(2,1)S(1)} %shard_map.154.refs_0_), channel_id=1, source_target_pairs={{0,48},{16,0},{32,16},{48,32},{1,49},{17,1},{33,17},{49,33},{2,50}... | collective-permute-start | bytes 1572872 | tf_op jit(solution)/shard_map/ppermute | solution.py:20
  15.5 2.2 %collective-permute-start.5 = (bf16[512,512]{1,0:T(8,128)(2,1)}, bf16[512,512]{1,0:T(8,128)(2,1)S(1)}, u32[]{:S(2)}, u32[]{:S(2)}) collective-permute-start(bf16[512,512]{1,0:T(8,128)(2,1)} %get-tuple-element.94.grads.refs_0_), channel_id=1, source_target_pairs={{0,1},{1,2},{2,3},{3,0},{4,5},{5,6},{6,7},{7,4},{8,9},{9,10},{10,1... | collective-permute-start | bytes 1572872 | tf_op jit(solution)/shard_map/ppermute | solution.py:20
  17.7 5.5 %collective-permute-done = bf16[64,2048]{1,0:T(8,128)(2,1)S(1)} collective-permute-done((bf16[64,2048]{1,0:T(8,128)(2,1)S(1)}, bf16[64,2048]{1,0:T(8,128)(2,1)S(1)}, u32[]{:S(2)}, u32[]{:S(2)}) %collective-permute-start) | collective-permute-done | bytes 262176 | tf_op jit(solution)/shard_map/ppermute | solution.py:306
  23.3 3.8 %collective-permute-start.9 = (bf16[64,2048]{1,0:T(8,128)(2,1)S(1)}, bf16[64,2048]{1,0:T(8,128)(2,1)}, u32[]{:S(2)}, u32[]{:S(2)}) collective-permute-start(bf16[64,2048]{1,0:T(8,128)(2,1)S(1)} %add_convert_fusion), channel_id=1, source_target_pairs={{0,192},{64,128},{128,64},{192,0},{1,193},{65,129},{129,65},{193,1... | collective-permute-start | bytes 786440 | tf_op jit(solution)/shard_map/ppermute | solution.py:312
  27.1 9.5 %shard_map.156 = (bf16[2,512,512]{2,1,0:T(8,128)(2,1)S(1)}, bf16[2,512,512]{2,1,0:T(8,128)(2,1)S(1)}, bf16[2,512,512]{2,1,0:T(8,128)(2,1)S(1)}, bf16[2,512,512]{2,1,0:T(8,128)(2,1)S(1)}, bf16[512,512]{1,0:T(8,128)(2,1)S(1)}) custom-call(s32[8]{0:T(128)S(1)} %get-tuple-element.143.where, bf16[512,8192]{1,0:T(8,128)(2,1)} %bitcast.33, ...), custom_call_target="tpu_custom_call" | custom-call | flops 4294967296 | tf_op jit(solution)/shard_map/pallas_call | solution.py:41
  37.4 2.8 %collective-permute-done.3.refs_3_ = bf16[512,512]{1,0:T(8,128)(2,1)S(1)} collective-permute-done((bf16[512,512]{1,0:T(8,128)(2,1)S(1)}, bf16[512,512]{1,0:T(8,128)(2,1)S(1)}, u32[]{:S(2)}, u32[]{:S(2)}) %collective-permute-start.3) | collective-permute-done | bytes 524320 | tf_op jit(solution)/shard_map/ppermute | solution.py:20
  42.6 1.9 %collective-permute-start.8 = (bf16[512,512]{1,0:T(8,128)(2,1)S(1)}, bf16[512,512]{1,0:T(8,128)(2,1)S(1)}, u32[]{:S(2)}, u32[]{:S(2)}) collective-permute-start(bf16[512,512]{1,0:T(8,128)(2,1)S(1)} %get-tuple-element.87.refs_4_), channel_id=1, source_target_pairs={{0,8},{8,0},{1,9},{9,1},{2,10},{10,2},{3,11},{11,3},{4,12},{12,4},... | collective-permute-start | bytes 1572872 | tf_op jit(solution)/shard_map/ppermute | solution.py:20
  44.5 3.2 %collective-permute-start.12 = (bf16[2,512,512]{2,1,0:T(8,128)(2,1)S(1)}, bf16[2,512,512]{2,1,0:T(8,128)(2,1)S(1)}, u32[]{:S(2)}, u32[]{:S(2)}) collective-permute-start(bf16[2,512,512]{2,1,0:T(8,128)(2,1)S(1)} %get-tuple-element.92), channel_id=1, source_target_pairs={{0,48},{16,0},{32,16},{48,32},{1,49},{17,1},{33,17},{49,33},{2,50}... | collective-permute-start | bytes 3145736 | tf_op jit(solution)/shard_map/ppermute | solution.py:20
  47.8 6.7 %collective-permute-done.6.refs_5_ = bf16[512,512]{1,0:T(8,128)(2,1)S(1)} collective-permute-done((bf16[512,512]{1,0:T(8,128)(2,1)S(1)}, bf16[512,512]{1,0:T(8,128)(2,1)S(1)}, u32[]{:S(2)}, u32[]{:S(2)}) %collective-permute-start.6) | collective-permute-done | bytes 524320 | tf_op jit(solution)/shard_map/ppermute | solution.py:20
  59.2 10.9 %collective-permute-done.10.refs_3_ = bf16[512,512]{1,0:T(8,128)(2,1)S(1)} collective-permute-done((bf16[512,512]{1,0:T(8,128)(2,1)S(1)}, bf16[512,512]{1,0:T(8,128)(2,1)S(1)}, u32[]{:S(2)}, u32[]{:S(2)}) %collective-permute-start.10) | collective-permute-done | bytes 524320 | tf_op jit(solution)/shard_map/ppermute | solution.py:20
  70.5 3.2 %collective-permute-start.19 = (bf16[512,512]{1,0:T(8,128)(2,1)S(1)}, bf16[512,512]{1,0:T(8,128)(2,1)S(1)}, u32[]{:S(2)}, u32[]{:S(2)}) collective-permute-start(bf16[512,512]{1,0:T(8,128)(2,1)S(1)} %get-tuple-element.102), channel_id=1, source_target_pairs={{0,48},{16,0},{32,16},{48,32},{1,49},{17,1},{33,17},{49,33},{2,50}... | collective-permute-start | bytes 1572872 | tf_op jit(solution)/shard_map/ppermute | solution.py:20
  73.7 1.9 %collective-permute-start.16 = (bf16[512,512]{1,0:T(8,128)(2,1)S(1)}, bf16[512,512]{1,0:T(8,128)(2,1)S(1)}, u32[]{:S(2)}, u32[]{:S(2)}) collective-permute-start(bf16[512,512]{1,0:T(8,128)(2,1)S(1)} %collective-permute-done.7.refs_2_), channel_id=1, source_target_pairs={{0,8},{8,0},{1,9},{9,1},{2,10},{10,2},{3,11},{11,3},{4,12},{12,4},... | collective-permute-start | bytes 1572872 | tf_op jit(solution)/shard_map/ppermute | solution.py:20
  76.1 2.3 %collective-permute-start.15 = (bf16[512,512]{1,0:T(8,128)(2,1)}, bf16[512,512]{1,0:T(8,128)(2,1)}, u32[]{:S(2)}, u32[]{:S(2)}) collective-permute-start(bf16[512,512]{1,0:T(8,128)(2,1)} %get-tuple-element.94.grads.refs_0_), channel_id=1, source_target_pairs={{0,2},{1,3},{2,0},{3,1},{4,6},{5,7},{6,4},{7,5},{8,10},{9,11},{10,... | collective-permute-start | bytes 1572872 | tf_op jit(solution)/shard_map/ppermute | solution.py:20
  78.4 5.1 %collective-permute-done.18.up = bf16[512,512]{1,0:T(8,128)(2,1)S(1)} collective-permute-done((bf16[512,512]{1,0:T(8,128)(2,1)S(1)}, bf16[512,512]{1,0:T(8,128)(2,1)S(1)}, u32[]{:S(2)}, u32[]{:S(2)}) %collective-permute-start.18) | collective-permute-done | bytes 524320 | tf_op jit(solution)/shard_map/ppermute | solution.py:20
  83.6 1.8 %collective-permute-start.17 = (bf16[512,512]{1,0:T(8,128)(2,1)S(1)}, bf16[512,512]{1,0:T(8,128)(2,1)S(1)}, u32[]{:S(2)}, u32[]{:S(2)}) collective-permute-start(bf16[512,512]{1,0:T(8,128)(2,1)S(1)} %collective-permute-done.10.refs_3_), channel_id=1, source_target_pairs={{0,8},{8,0},{1,9},{9,1},{2,10},{10,2},{3,11},{11,3},{4,12},{12,4},... | collective-permute-start | bytes 1572872 | tf_op jit(solution)/shard_map/ppermute | solution.py:20
  85.4 2.9 %shard_map.159 = (f32[512,512]{1,0:T(8,128)S(1)}, f32[512,512]{1,0:T(8,128)S(1)}) custom-call(s32[1]{0:T(128)} %constant.75.clone.1._, bf16[512,512]{1,0:T(8,128)(2,1)} %get-tuple-element.94.grads.refs_0_, bf16[512,512]{1,0:T(8,128)(2,1)} %copy-done.15, bf16[512,512]{1,0:T(8,128)(2,1)} %copy-done.8, bf16[512,512]{1,0:T(8,128)(2,1)S(1)} %collective-permute-done.20.refs_3_, ...), custom_call_target="tpu_custom_call" | custom-call | flops 1073741824 | tf_op jit(solution)/shard_map/pallas_call | solution.py:41
  90.3 2.9 %shard_map.160 = (f32[512,512]{1,0:T(8,128)S(1)}, f32[512,512]{1,0:T(8,128)S(1)}) custom-call(s32[1]{0:T(128)} %constant.75.clone.1._, bf16[512,512]{1,0:T(8,128)(2,1)} %get-tuple-element.94.grads.refs_0_, bf16[512,512]{1,0:T(8,128)(2,1)} %copy-done.15, bf16[512,512]{1,0:T(8,128)(2,1)} %copy-done.8, bf16[512,512]{1,0:T(8,128)(2,1)S(1)} %collective-permute-done.20.refs_3_, ...), custom_call_target="tpu_custom_call" | custom-call | flops 1073741824 | tf_op jit(solution)/shard_map/pallas_call | solution.py:41
  96.0 3.3 %collective-permute-done.14.refs_0_ = bf16[512,512]{1,0:T(8,128)(2,1)} collective-permute-done((bf16[512,512]{1,0:T(8,128)(2,1)}, bf16[512,512]{1,0:T(8,128)(2,1)}, u32[]{:S(2)}, u32[]{:S(2)}) %collective-permute-start.14) | collective-permute-done | bytes 524320 | tf_op jit(solution)/shard_map/ppermute | solution.py:20
  102.8 4.8 %shard_map.162._ = bf16[512,2048]{1,0:T(8,128)(2,1)} custom-call(s32[2]{0:T(128)S(1)} %pad_add_fusion.1.where, bf16[512,512]{1,0:T(8,128)(2,1)} %collective-permute-done.14.refs_0_, bf16[512,512]{1,0:T(8,128)(2,1)} %collective-permute-done.15.refs_1_, bf16[512,512]{1,0:T(8,128)(2,1)} %copy-done.11, bf16[512,512]{1,0:T(8,128)(2,1)S(1)} %collective-permute-done.10.refs_3_, ...), custom_call_target="tpu_custom_call" | custom-call | tf_op jit(solution)/shard_map/pallas_call | solution.py:41
  107.6 3.9 %shard_map.163 = (bf16[512,512]{1,0:T(8,128)(2,1)S(1)}, bf16[512,512]{1,0:T(8,128)(2,1)S(1)}) custom-call(s32[1]{0:T(128)} %constant.75.clone.1._, bf16[512,512]{1,0:T(8,128)(2,1)} %collective-permute-done.21.refs_0_, bf16[512,512]{1,0:T(8,128)(2,1)} %collective-permute-done.22.refs_1_, bf16[512,512]{1,0:T(8,128)(2,1)} %copy-done.11, ...), custom_call_target="tpu_custom_call" | custom-call | tf_op jit(solution)/shard_map/pallas_call | solution.py:41
  112.1 2.3 %fusion = (f32[64,2048]{1,0:T(8,128)}, f32[64,2048]{1,0:T(8,128)}, f32[64,2048]{1,0:T(8,128)}) fusion(f32[1,64,2048]{2,1,0:T(8,128)S(1)} %copy-done.10, f32[64,2048]{1,0:T(8,128)S(1)} %copy-done.13, f32[64,2048]{1,0:T(8,128)S(1)} %copy-done.14, bf16[64,2048]{1,0:T(8,128)(2,1)} %collective-permute-done.9, bf16[64,2048]{1,0:T(8,128)(2,1)S(1)} %add_convert_fusion, ...), kind=kLoop, calls=%fused_computation.2 | loop fusion | flops 1703936 | bytes 3670020 | tf_op jit(solution)/shard_map/add | solution.py:351
  114.7 2.0 %collective-permute-done.25.received = bf16[512,512]{1,0:T(8,128)(2,1)S(1)} collective-permute-done((bf16[512,512]{1,0:T(8,128)(2,1)}, bf16[512,512]{1,0:T(8,128)(2,1)S(1)}, u32[]{:S(2)}, u32[]{:S(2)}) %collective-permute-start.25) | collective-permute-done | bytes 524320 | tf_op jit(solution)/shard_map/ppermute | solution.py:20
  (89 shorter events, 21.9 us)
Async XLA Ops:
  7.2 8.3 %collective-permute-start.4 = (bf16[9,512,512]{2,1,0:T(8,128)(2,1)}, bf16[9,512,512]{2,1,0:T(8,128)(2,1)}, u32[]{:S(2)}, u32[]{:S(2)}) collective-permute-start(bf16[9,512,512]{2,1,0:T(8,128)(2,1)} %get-tuple-element.76), channel_id=1, source_target_pairs={{0,4},{4,0},{1,5},{5,1},{2,6},{6,2},{3,7},{7,3},{8,12},{12,8},{9,1... | collective-permute-start | bytes 14155784 | tf_op jit(solution)/shard_map/ppermute | solution.py:20
  7.3 15.9 %collective-permute-start = (bf16[64,2048]{1,0:T(8,128)(2,1)S(1)}, bf16[64,2048]{1,0:T(8,128)(2,1)S(1)}, u32[]{:S(2)}, u32[]{:S(2)}) collective-permute-start(bf16[64,2048]{1,0:T(8,128)(2,1)S(1)} %bitcast_convert_fusion), channel_id=1, source_target_pairs={{0,64},{64,0},{128,192},{192,128},{1,65},{65,1},{129,193},{193,129... | collective-permute-start | bytes 786440 | tf_op jit(solution)/shard_map/ppermute | solution.py:306
  10.7 26.7 %collective-permute-start.1 = (bf16[512,512]{1,0:T(8,128)(2,1)S(1)}, bf16[512,512]{1,0:T(8,128)(2,1)S(1)}, u32[]{:S(2)}, u32[]{:S(2)}) collective-permute-start(bf16[512,512]{1,0:T(8,128)(2,1)S(1)} %shard_map.154.refs_0_), channel_id=1, source_target_pairs={{0,48},{16,0},{32,16},{48,32},{1,49},{17,1},{33,17},{49,33},{2,50}... | collective-permute-start | bytes 1572872 | tf_op jit(solution)/shard_map/ppermute | solution.py:20
  13.7 23.7 %collective-permute-start.2 = (bf16[512,512]{1,0:T(8,128)(2,1)S(1)}, bf16[512,512]{1,0:T(8,128)(2,1)S(1)}, u32[]{:S(2)}, u32[]{:S(2)}) collective-permute-start(bf16[512,512]{1,0:T(8,128)(2,1)S(1)} %shard_map.154.refs_0_), channel_id=1, source_target_pairs={{0,32},{16,48},{32,0},{48,16},{1,33},{17,49},{33,1},{49,17},{2,34}... | collective-permute-start | bytes 1572872 | tf_op jit(solution)/shard_map/ppermute | solution.py:20
  14.3 25.9 %collective-permute-start.3 = (bf16[512,512]{1,0:T(8,128)(2,1)S(1)}, bf16[512,512]{1,0:T(8,128)(2,1)S(1)}, u32[]{:S(2)}, u32[]{:S(2)}) collective-permute-start(bf16[512,512]{1,0:T(8,128)(2,1)S(1)} %shard_map.154.refs_0_), channel_id=1, source_target_pairs={{0,16},{16,32},{32,48},{48,0},{1,17},{17,33},{33,49},{49,1},{2,18}... | collective-permute-start | bytes 1572872 | tf_op jit(solution)/shard_map/ppermute | solution.py:20
  15.5 24.7 %collective-permute-start.5 = (bf16[512,512]{1,0:T(8,128)(2,1)}, bf16[512,512]{1,0:T(8,128)(2,1)S(1)}, u32[]{:S(2)}, u32[]{:S(2)}) collective-permute-start(bf16[512,512]{1,0:T(8,128)(2,1)} %get-tuple-element.94.grads.refs_0_), channel_id=1, source_target_pairs={{0,1},{1,2},{2,3},{3,0},{4,5},{5,6},{6,7},{7,4},{8,9},{9,10},{10,1... | collective-permute-start | bytes 1572872 | tf_op jit(solution)/shard_map/ppermute | solution.py:20
  23.3 21.2 %collective-permute-start.9 = (bf16[64,2048]{1,0:T(8,128)(2,1)S(1)}, bf16[64,2048]{1,0:T(8,128)(2,1)}, u32[]{:S(2)}, u32[]{:S(2)}) collective-permute-start(bf16[64,2048]{1,0:T(8,128)(2,1)S(1)} %add_convert_fusion), channel_id=1, source_target_pairs={{0,192},{64,128},{128,64},{192,0},{1,193},{65,129},{129,65},{193,1... | collective-permute-start | bytes 786440 | tf_op jit(solution)/shard_map/ppermute | solution.py:312
  40.5 13.9 %collective-permute-start.6 = (bf16[512,512]{1,0:T(8,128)(2,1)S(1)}, bf16[512,512]{1,0:T(8,128)(2,1)S(1)}, u32[]{:S(2)}, u32[]{:S(2)}) collective-permute-start(bf16[512,512]{1,0:T(8,128)(2,1)S(1)} %get-tuple-element.85), channel_id=1, source_target_pairs={{0,1},{1,2},{2,3},{3,0},{4,5},{5,6},{6,7},{7,4},{8,9},{9,10},{10,1... | collective-permute-start | bytes 1572872 | tf_op jit(solution)/shard_map/ppermute | solution.py:20
  41.1 14.8 %collective-permute-start.7 = (bf16[512,512]{1,0:T(8,128)(2,1)S(1)}, bf16[512,512]{1,0:T(8,128)(2,1)S(1)}, u32[]{:S(2)}, u32[]{:S(2)}) collective-permute-start(bf16[512,512]{1,0:T(8,128)(2,1)S(1)} %get-tuple-element.86), channel_id=1, source_target_pairs={{0,3},{1,0},{2,1},{3,2},{4,7},{5,4},{6,5},{7,6},{8,11},{9,8},{10,9... | collective-permute-start | bytes 1572872 | tf_op jit(solution)/shard_map/ppermute | solution.py:20
  42.6 13.5 %collective-permute-start.8 = (bf16[512,512]{1,0:T(8,128)(2,1)S(1)}, bf16[512,512]{1,0:T(8,128)(2,1)S(1)}, u32[]{:S(2)}, u32[]{:S(2)}) collective-permute-start(bf16[512,512]{1,0:T(8,128)(2,1)S(1)} %get-tuple-element.87.refs_4_), channel_id=1, source_target_pairs={{0,8},{8,0},{1,9},{9,1},{2,10},{10,2},{3,11},{11,3},{4,12},{12,4},... | collective-permute-start | bytes 1572872 | tf_op jit(solution)/shard_map/ppermute | solution.py:20
  44.5 25.6 %collective-permute-start.11 = (bf16[2,512,512]{2,1,0:T(8,128)(2,1)S(1)}, bf16[2,512,512]{2,1,0:T(8,128)(2,1)S(1)}, u32[]{:S(2)}, u32[]{:S(2)}) collective-permute-start(bf16[2,512,512]{2,1,0:T(8,128)(2,1)S(1)} %get-tuple-element.91), channel_id=1, source_target_pairs={{0,16},{16,32},{32,48},{48,0},{1,17},{17,33},{33,49},{49,1},{2,18}... | collective-permute-start | bytes 3145736 | tf_op jit(solution)/shard_map/ppermute | solution.py:20
  44.5 25.6 %collective-permute-start.12 = (bf16[2,512,512]{2,1,0:T(8,128)(2,1)S(1)}, bf16[2,512,512]{2,1,0:T(8,128)(2,1)S(1)}, u32[]{:S(2)}, u32[]{:S(2)}) collective-permute-start(bf16[2,512,512]{2,1,0:T(8,128)(2,1)S(1)} %get-tuple-element.92), channel_id=1, source_target_pairs={{0,48},{16,0},{32,16},{48,32},{1,49},{17,1},{33,17},{49,33},{2,50}... | collective-permute-start | bytes 3145736 | tf_op jit(solution)/shard_map/ppermute | solution.py:20
  56.1 14.1 %collective-permute-start.10 = (bf16[512,512]{1,0:T(8,128)(2,1)S(1)}, bf16[512,512]{1,0:T(8,128)(2,1)S(1)}, u32[]{:S(2)}, u32[]{:S(2)}) collective-permute-start(bf16[512,512]{1,0:T(8,128)(2,1)S(1)} %get-tuple-element.90), channel_id=1, source_target_pairs={{0,2},{1,3},{2,0},{3,1},{4,6},{5,7},{6,4},{7,5},{8,10},{9,11},{10,... | collective-permute-start | bytes 1572872 | tf_op jit(solution)/shard_map/ppermute | solution.py:20
  57.5 12.6 %collective-permute-start.13 = (bf16[512,512]{1,0:T(8,128)(2,1)S(1)}, bf16[512,512]{1,0:T(8,128)(2,1)S(1)}, u32[]{:S(2)}, u32[]{:S(2)}) collective-permute-start(bf16[512,512]{1,0:T(8,128)(2,1)S(1)} %collective-permute-done.6.refs_5_), channel_id=1, source_target_pairs={{0,8},{8,0},{1,9},{9,1},{2,10},{10,2},{3,11},{11,3},{4,12},{12,4},... | collective-permute-start | bytes 1572872 | tf_op jit(solution)/shard_map/ppermute | solution.py:20
  59.2 16.9 %collective-permute-start.20 = (bf16[512,512]{1,0:T(8,128)(2,1)S(1)}, bf16[512,512]{1,0:T(8,128)(2,1)S(1)}, u32[]{:S(2)}, u32[]{:S(2)}) collective-permute-start(bf16[512,512]{1,0:T(8,128)(2,1)S(1)} %collective-permute-done.5.refs_1_), channel_id=1, source_target_pairs={{0,4},{4,0},{1,5},{5,1},{2,6},{6,2},{3,7},{7,3},{8,12},{12,8},{9,1... | collective-permute-start | bytes 1572872 | tf_op jit(solution)/shard_map/ppermute | solution.py:20
  70.4 13.2 %collective-permute-start.18 = (bf16[512,512]{1,0:T(8,128)(2,1)S(1)}, bf16[512,512]{1,0:T(8,128)(2,1)S(1)}, u32[]{:S(2)}, u32[]{:S(2)}) collective-permute-start(bf16[512,512]{1,0:T(8,128)(2,1)S(1)} %get-tuple-element.101), channel_id=1, source_target_pairs={{0,16},{16,32},{32,48},{48,0},{1,17},{17,33},{33,49},{49,1},{2,18}... | collective-permute-start | bytes 1572872 | tf_op jit(solution)/shard_map/ppermute | solution.py:20
  70.5 23.7 %collective-permute-start.19 = (bf16[512,512]{1,0:T(8,128)(2,1)S(1)}, bf16[512,512]{1,0:T(8,128)(2,1)S(1)}, u32[]{:S(2)}, u32[]{:S(2)}) collective-permute-start(bf16[512,512]{1,0:T(8,128)(2,1)S(1)} %get-tuple-element.102), channel_id=1, source_target_pairs={{0,48},{16,0},{32,16},{48,32},{1,49},{17,1},{33,17},{49,33},{2,50}... | collective-permute-start | bytes 1572872 | tf_op jit(solution)/shard_map/ppermute | solution.py:20
  73.7 22.3 %collective-permute-start.16 = (bf16[512,512]{1,0:T(8,128)(2,1)S(1)}, bf16[512,512]{1,0:T(8,128)(2,1)S(1)}, u32[]{:S(2)}, u32[]{:S(2)}) collective-permute-start(bf16[512,512]{1,0:T(8,128)(2,1)S(1)} %collective-permute-done.7.refs_2_), channel_id=1, source_target_pairs={{0,8},{8,0},{1,9},{9,1},{2,10},{10,2},{3,11},{11,3},{4,12},{12,4},... | collective-permute-start | bytes 1572872 | tf_op jit(solution)/shard_map/ppermute | solution.py:20
  75.6 23.7 %collective-permute-start.14 = (bf16[512,512]{1,0:T(8,128)(2,1)}, bf16[512,512]{1,0:T(8,128)(2,1)}, u32[]{:S(2)}, u32[]{:S(2)}) collective-permute-start(bf16[512,512]{1,0:T(8,128)(2,1)} %get-tuple-element.94.grads.refs_0_), channel_id=1, source_target_pairs={{0,3},{1,0},{2,1},{3,2},{4,7},{5,4},{6,5},{7,6},{8,11},{9,8},{10,9... | collective-permute-start | bytes 1572872 | tf_op jit(solution)/shard_map/ppermute | solution.py:20
  76.1 23.2 %collective-permute-start.15 = (bf16[512,512]{1,0:T(8,128)(2,1)}, bf16[512,512]{1,0:T(8,128)(2,1)}, u32[]{:S(2)}, u32[]{:S(2)}) collective-permute-start(bf16[512,512]{1,0:T(8,128)(2,1)} %get-tuple-element.94.grads.refs_0_), channel_id=1, source_target_pairs={{0,2},{1,3},{2,0},{3,1},{4,6},{5,7},{6,4},{7,5},{8,10},{9,11},{10,... | collective-permute-start | bytes 1572872 | tf_op jit(solution)/shard_map/ppermute | solution.py:20
  83.6 15.7 %collective-permute-start.17 = (bf16[512,512]{1,0:T(8,128)(2,1)S(1)}, bf16[512,512]{1,0:T(8,128)(2,1)S(1)}, u32[]{:S(2)}, u32[]{:S(2)}) collective-permute-start(bf16[512,512]{1,0:T(8,128)(2,1)S(1)} %collective-permute-done.10.refs_3_), channel_id=1, source_target_pairs={{0,8},{8,0},{1,9},{9,1},{2,10},{10,2},{3,11},{11,3},{4,12},{12,4},... | collective-permute-start | bytes 1572872 | tf_op jit(solution)/shard_map/ppermute | solution.py:20
  99.3 8.3 %collective-permute-start.21 = (bf16[512,512]{1,0:T(8,128)(2,1)}, bf16[512,512]{1,0:T(8,128)(2,1)}, u32[]{:S(2)}, u32[]{:S(2)}) collective-permute-start(bf16[512,512]{1,0:T(8,128)(2,1)} %collective-permute-done.14.refs_0_), channel_id=1, source_target_pairs={{0,4},{4,0},{1,5},{5,1},{2,6},{6,2},{3,7},{7,3},{8,12},{12,8},{9,1... | collective-permute-start | bytes 1572872 | tf_op jit(solution)/shard_map/ppermute | solution.py:20
  99.4 8.2 %collective-permute-start.22 = (bf16[512,512]{1,0:T(8,128)(2,1)}, bf16[512,512]{1,0:T(8,128)(2,1)}, u32[]{:S(2)}, u32[]{:S(2)}) collective-permute-start(bf16[512,512]{1,0:T(8,128)(2,1)} %collective-permute-done.15.refs_1_), channel_id=1, source_target_pairs={{0,4},{4,0},{1,5},{5,1},{2,6},{6,2},{3,7},{7,3},{8,12},{12,8},{9,1... | collective-permute-start | bytes 1572872 | tf_op jit(solution)/shard_map/ppermute | solution.py:20
  102.6 14.2 %collective-permute-start.25 = (bf16[512,512]{1,0:T(8,128)(2,1)}, bf16[512,512]{1,0:T(8,128)(2,1)S(1)}, u32[]{:S(2)}, u32[]{:S(2)}) collective-permute-start(bf16[512,512]{1,0:T(8,128)(2,1)} %copy-done.6), channel_id=1, source_target_pairs={{0,8},{8,0},{1,9},{9,1},{2,10},{10,2},{3,11},{11,3},{4,12},{12,4},... | collective-permute-start | bytes 1572872 | tf_op jit(solution)/shard_map/ppermute | solution.py:20
  (22 other events, 290.0 us)

commit v4 on v3

--- a/solution.py
+++ b/solution.py
@@ -221,25 +221,6 @@
     return call(back_kernel, where, ins, [like(tokens, 4 * width)], scratch, far=(2, 4, 6, 7, 8))[0]
 
 
-def place_kernel(where, a, b, _, out, sems):
-    width = a.shape[1]
-    copies = [started(block, column(out, where[k], width), sems.at[k]) for k, block in enumerate((a, b))]
-    for copy in copies:
-        copy.wait()
-
-
-def place(where, blocks, back):
-    return call(
-        place_kernel,
-        where,
-        [*blocks, back],
-        [like(*back.shape)],
-        [pltpu.SemaphoreType.DMA((2,))],
-        far=(2, 3),
-        aliases={3: 0},
-    )[0]
-
-
 def relay_kernel(_, rest, up, down, first, second):
     first[...] = (rest[0].astype(f32) + up[0].astype(f32)).astype(bf16)
     second[...] = (rest[1].astype(f32) + down[0].astype(f32)).astype(bf16)
@@ -253,25 +234,29 @@
     out[...] = (own[1].astype(f32) + up[1].astype(f32) + down[...].astype(f32)).T
 
 
-def final_kernel(_, part, received, key_out, value_out, k_buf, v_buf, sems):
+def final_kernel(where, part, received, a, b, _, key_out, value_out, out, k_buf, v_buf, sems):
+    cols = a.shape[1]
+    copies = [started(block, column(out, where[k], cols), sems.at[k]) for k, block in enumerate((a, b))]
     width = k_buf.shape[1]
     k_buf[...] = part[:, :width] + received[:width].astype(f32).T
-    first = started(k_buf, key_out, sems.at[0])
+    copies.append(started(k_buf, key_out, sems.at[2]))
     v_buf[...] = part[:, width:] + received[width:].astype(f32).T
-    started(v_buf, value_out, sems.at[1]).wait()
-    first.wait()
-
-
-def final_sum(none, part, received):
+    copies.append(started(v_buf, value_out, sems.at[3]))
+    for copy in copies:
+        copy.wait()
+
+
+def finish(where, part, received, blocks, back):
     rows, cols = received.shape
     half = (cols, rows // 2)
     return call(
         final_kernel,
-        none,
-        [part, received],
-        [like(*half, dtype=f32)] * 2,
-        [pltpu.VMEM(half, f32), pltpu.VMEM(half, f32), pltpu.SemaphoreType.DMA((2,))],
-        far=(2, 3),
+        where,
+        [part, received, *blocks, back],
+        [like(*half, dtype=f32)] * 2 + [like(*back.shape)],
+        [pltpu.VMEM(half, f32), pltpu.VMEM(half, f32), pltpu.SemaphoreType.DMA((4,))],
+        far=(4, 5, 6, 7),
+        aliases={5: 2},
     )
 
 
@@ -352,9 +337,8 @@
     fresh_global, fresh_momentum, fresh_local, back, loose, mine, received = fence(
         (fresh_global, fresh_momentum, fresh_local, back, loose, mine, received)
     )
-    back = place(jnp.stack([iz * 2 + 1 - ic, (1 - iz) * 2 + 1 - ic]), loose, back)
-    wgrad_k, wgrad_v = final_sum(none, mine, received)
-
+    places = jnp.stack([iz * 2 + 1 - ic, (1 - iz) * 2 + 1 - ic])
+    wgrad_k, wgrad_v, back = finish(places, mine, received, loose, back)
     return (
         back[None],
         wgrad_k[None],

time: 120 us -> 119 us (level)
    pallas_call x13 -> x12, Pallas kernels: 34 us -> 33.3 us  [call(): pl.pallas_call(kernel, out_shape=[space(a.shape, a.dtype) for a, space in...]
where the time goes in v4:
time: 119 us
  waiting for transfers between devices  37.3 us (31%)
  starting transfers between devices  35.8 us (30%)
  Pallas kernels  33.3 us (28%)
  local copies, waits for them, and re-layouts  6.42 us (5%)
  other arithmetic  3.13 us (3%)
  between operations  3.01 us (3%)
    pallas_call x12, Pallas kernels, call(): pl.pallas_call(kernel, out_shape=[space(a.shape, a.dtype) for a, space in...  33.3 us
    ppermute x24, waiting for transfers between devices, shift(): return lax.ppermute(a, axis, [(i, (i + by) % n) for i in range(n)])  31.7 us
    ppermute x24, starting transfers between devices, shift(): return lax.ppermute(a, axis, [(i, (i + by) % n) for i in range(n)])  28.6 us
    unnamed x40, local copies, waits for them, and re-layouts  6.34 us
    ppermute x1, waiting for transfers between devices, local(): pair_sib = lax.ppermute(sent, 'r', [(k, k ^ 1) for k in range(4)])  5.53 us
    ppermute x1, starting transfers between devices, local(): pair_sib = lax.ppermute(pair, 'r', [(k, k ^ 3) for k in range(4)])  3.83 us
    ppermute x1, starting transfers between devices, local(): pair_sib = lax.ppermute(sent, 'r', [(k, k ^ 1) for k in range(4)])  3.36 us
  transfers between devices with their start and end apart: 26, of which 10 were waited for; matrix products, arithmetic and copies ran while one was open for 3% of the time, Pallas kernels for 21%

profile of v4, /device:TPU:6, one launch (start us, length us, event | category | flops | bytes accessed | tf_op | source)
XLA Modules:
  0.0 118.9 jit_solution(10948941857473276633)
XLA Ops:
  1.9 5.3 %shard_map.155 = (bf16[512,512]{1,0:T(8,128)(2,1)}, bf16[9,512,512]{2,1,0:T(8,128)(2,1)}) custom-call(s32[8]{0:T(128)S(1)} %get-tuple-element.146.where, bf16[512,8192]{1,0:T(8,128)(2,1)} %bitcast.32, bf16[512,256]{1,0:T(8,128)(2,1)} %bitcast.36, bf16[512,256]{1,0:T(8,128)(2,1)} %bitcast.37), custom_call_target="tpu_custom_call" | custom-call | tf_op jit(solution)/shard_map/pallas_call | solution.py:41
  7.3 3.4 %collective-permute-start = (bf16[64,2048]{1,0:T(8,128)(2,1)S(1)}, bf16[64,2048]{1,0:T(8,128)(2,1)S(1)}, u32[]{:S(2)}, u32[]{:S(2)}) collective-permute-start(bf16[64,2048]{1,0:T(8,128)(2,1)S(1)} %bitcast_convert_fusion), channel_id=1, source_target_pairs={{0,64},{64,0},{128,192},{192,128},{1,65},{65,1},{129,193},{193,129... | collective-permute-start | bytes 786440 | tf_op jit(solution)/shard_map/ppermute | solution.py:291
  10.7 3.0 %collective-permute-start.1 = (bf16[512,512]{1,0:T(8,128)(2,1)S(1)}, bf16[512,512]{1,0:T(8,128)(2,1)S(1)}, u32[]{:S(2)}, u32[]{:S(2)}) collective-permute-start(bf16[512,512]{1,0:T(8,128)(2,1)S(1)} %shard_map.154.refs_0_), channel_id=1, source_target_pairs={{0,48},{16,0},{32,16},{48,32},{1,49},{17,1},{33,17},{49,33},{2,50}... | collective-permute-start | bytes 1572872 | tf_op jit(solution)/shard_map/ppermute | solution.py:20
  15.5 2.2 %collective-permute-start.5 = (bf16[512,512]{1,0:T(8,128)(2,1)}, bf16[512,512]{1,0:T(8,128)(2,1)S(1)}, u32[]{:S(2)}, u32[]{:S(2)}) collective-permute-start(bf16[512,512]{1,0:T(8,128)(2,1)} %get-tuple-element.95.grads.refs_0_), channel_id=1, source_target_pairs={{0,1},{1,2},{2,3},{3,0},{4,5},{5,6},{6,7},{7,4},{8,9},{9,10},{10,1... | collective-permute-start | bytes 1572872 | tf_op jit(solution)/shard_map/ppermute | solution.py:20
  17.7 5.5 %collective-permute-done = bf16[64,2048]{1,0:T(8,128)(2,1)S(1)} collective-permute-done((bf16[64,2048]{1,0:T(8,128)(2,1)S(1)}, bf16[64,2048]{1,0:T(8,128)(2,1)S(1)}, u32[]{:S(2)}, u32[]{:S(2)}) %collective-permute-start) | collective-permute-done | bytes 262176 | tf_op jit(solution)/shard_map/ppermute | solution.py:291
  23.3 3.8 %collective-permute-start.9 = (bf16[64,2048]{1,0:T(8,128)(2,1)S(1)}, bf16[64,2048]{1,0:T(8,128)(2,1)}, u32[]{:S(2)}, u32[]{:S(2)}) collective-permute-start(bf16[64,2048]{1,0:T(8,128)(2,1)S(1)} %add_convert_fusion), channel_id=1, source_target_pairs={{0,192},{64,128},{128,64},{192,0},{1,193},{65,129},{129,65},{193,1... | collective-permute-start | bytes 786440 | tf_op jit(solution)/shard_map/ppermute | solution.py:297
  27.1 9.5 %shard_map.156 = (bf16[2,512,512]{2,1,0:T(8,128)(2,1)S(1)}, bf16[2,512,512]{2,1,0:T(8,128)(2,1)S(1)}, bf16[2,512,512]{2,1,0:T(8,128)(2,1)S(1)}, bf16[2,512,512]{2,1,0:T(8,128)(2,1)S(1)}, bf16[512,512]{1,0:T(8,128)(2,1)S(1)}) custom-call(s32[8]{0:T(128)S(1)} %get-tuple-element.145.where, bf16[512,8192]{1,0:T(8,128)(2,1)} %bitcast.33, ...), custom_call_target="tpu_custom_call" | custom-call | flops 4294967296 | tf_op jit(solution)/shard_map/pallas_call | solution.py:41
  37.4 2.8 %collective-permute-done.3.refs_3_ = bf16[512,512]{1,0:T(8,128)(2,1)S(1)} collective-permute-done((bf16[512,512]{1,0:T(8,128)(2,1)S(1)}, bf16[512,512]{1,0:T(8,128)(2,1)S(1)}, u32[]{:S(2)}, u32[]{:S(2)}) %collective-permute-start.3) | collective-permute-done | bytes 524320 | tf_op jit(solution)/shard_map/ppermute | solution.py:20
  42.6 1.9 %collective-permute-start.8 = (bf16[512,512]{1,0:T(8,128)(2,1)S(1)}, bf16[512,512]{1,0:T(8,128)(2,1)S(1)}, u32[]{:S(2)}, u32[]{:S(2)}) collective-permute-start(bf16[512,512]{1,0:T(8,128)(2,1)S(1)} %get-tuple-element.88.refs_4_), channel_id=1, source_target_pairs={{0,8},{8,0},{1,9},{9,1},{2,10},{10,2},{3,11},{11,3},{4,12},{12,4},... | collective-permute-start | bytes 1572872 | tf_op jit(solution)/shard_map/ppermute | solution.py:20
  44.5 3.2 %collective-permute-start.12 = (bf16[2,512,512]{2,1,0:T(8,128)(2,1)S(1)}, bf16[2,512,512]{2,1,0:T(8,128)(2,1)S(1)}, u32[]{:S(2)}, u32[]{:S(2)}) collective-permute-start(bf16[2,512,512]{2,1,0:T(8,128)(2,1)S(1)} %get-tuple-element.93), channel_id=1, source_target_pairs={{0,48},{16,0},{32,16},{48,32},{1,49},{17,1},{33,17},{49,33},{2,50}... | collective-permute-start | bytes 3145736 | tf_op jit(solution)/shard_map/ppermute | solution.py:20
  47.8 6.7 %collective-permute-done.6.refs_5_ = bf16[512,512]{1,0:T(8,128)(2,1)S(1)} collective-permute-done((bf16[512,512]{1,0:T(8,128)(2,1)S(1)}, bf16[512,512]{1,0:T(8,128)(2,1)S(1)}, u32[]{:S(2)}, u32[]{:S(2)}) %collective-permute-start.6) | collective-permute-done | bytes 524320 | tf_op jit(solution)/shard_map/ppermute | solution.py:20
  59.2 10.9 %collective-permute-done.10.refs_3_ = bf16[512,512]{1,0:T(8,128)(2,1)S(1)} collective-permute-done((bf16[512,512]{1,0:T(8,128)(2,1)S(1)}, bf16[512,512]{1,0:T(8,128)(2,1)S(1)}, u32[]{:S(2)}, u32[]{:S(2)}) %collective-permute-start.10) | collective-permute-done | bytes 524320 | tf_op jit(solution)/shard_map/ppermute | solution.py:20
  70.5 3.2 %collective-permute-start.19 = (bf16[512,512]{1,0:T(8,128)(2,1)S(1)}, bf16[512,512]{1,0:T(8,128)(2,1)S(1)}, u32[]{:S(2)}, u32[]{:S(2)}) collective-permute-start(bf16[512,512]{1,0:T(8,128)(2,1)S(1)} %get-tuple-element.103), channel_id=1, source_target_pairs={{0,48},{16,0},{32,16},{48,32},{1,49},{17,1},{33,17},{49,33},{2,50}... | collective-permute-start | bytes 1572872 | tf_op jit(solution)/shard_map/ppermute | solution.py:20
  73.7 1.9 %collective-permute-start.16 = (bf16[512,512]{1,0:T(8,128)(2,1)S(1)}, bf16[512,512]{1,0:T(8,128)(2,1)S(1)}, u32[]{:S(2)}, u32[]{:S(2)}) collective-permute-start(bf16[512,512]{1,0:T(8,128)(2,1)S(1)} %collective-permute-done.7.refs_2_), channel_id=1, source_target_pairs={{0,8},{8,0},{1,9},{9,1},{2,10},{10,2},{3,11},{11,3},{4,12},{12,4},... | collective-permute-start | bytes 1572872 | tf_op jit(solution)/shard_map/ppermute | solution.py:20
  76.1 2.3 %collective-permute-start.15 = (bf16[512,512]{1,0:T(8,128)(2,1)}, bf16[512,512]{1,0:T(8,128)(2,1)}, u32[]{:S(2)}, u32[]{:S(2)}) collective-permute-start(bf16[512,512]{1,0:T(8,128)(2,1)} %get-tuple-element.95.grads.refs_0_), channel_id=1, source_target_pairs={{0,2},{1,3},{2,0},{3,1},{4,6},{5,7},{6,4},{7,5},{8,10},{9,11},{10,... | collective-permute-start | bytes 1572872 | tf_op jit(solution)/shard_map/ppermute | solution.py:20
  78.4 5.1 %collective-permute-done.18.up = bf16[512,512]{1,0:T(8,128)(2,1)S(1)} collective-permute-done((bf16[512,512]{1,0:T(8,128)(2,1)S(1)}, bf16[512,512]{1,0:T(8,128)(2,1)S(1)}, u32[]{:S(2)}, u32[]{:S(2)}) %collective-permute-start.18) | collective-permute-done | bytes 524320 | tf_op jit(solution)/shard_map/ppermute | solution.py:20
  85.4 2.9 %shard_map.159 = (f32[512,512]{1,0:T(8,128)S(1)}, f32[512,512]{1,0:T(8,128)S(1)}) custom-call(s32[1]{0:T(128)} %constant.75.clone.1._, bf16[512,512]{1,0:T(8,128)(2,1)} %get-tuple-element.95.grads.refs_0_, bf16[512,512]{1,0:T(8,128)(2,1)} %copy-done.15, bf16[512,512]{1,0:T(8,128)(2,1)} %copy-done.8, bf16[512,512]{1,0:T(8,128)(2,1)S(1)} %collective-permute-done.20.refs_3_, ...), custom_call_target="tpu_custom_call" | custom-call | flops 1073741824 | tf_op jit(solution)/shard_map/pallas_call | solution.py:41
  90.3 2.9 %shard_map.160 = (f32[512,512]{1,0:T(8,128)S(1)}, f32[512,512]{1,0:T(8,128)S(1)}) custom-call(s32[1]{0:T(128)} %constant.75.clone.1._, bf16[512,512]{1,0:T(8,128)(2,1)} %get-tuple-element.95.grads.refs_0_, bf16[512,512]{1,0:T(8,128)(2,1)} %copy-done.15, bf16[512,512]{1,0:T(8,128)(2,1)} %copy-done.8, bf16[512,512]{1,0:T(8,128)(2,1)S(1)} %collective-permute-done.20.refs_3_, ...), custom_call_target="tpu_custom_call" | custom-call | flops 1073741824 | tf_op jit(solution)/shard_map/pallas_call | solution.py:41
  97.0 2.4 %collective-permute-done.14.refs_0_ = bf16[512,512]{1,0:T(8,128)(2,1)} collective-permute-done((bf16[512,512]{1,0:T(8,128)(2,1)}, bf16[512,512]{1,0:T(8,128)(2,1)}, u32[]{:S(2)}, u32[]{:S(2)}) %collective-permute-start.14) | collective-permute-done | bytes 524320 | tf_op jit(solution)/shard_map/ppermute | solution.py:20
  102.8 4.8 %shard_map.162._ = bf16[512,2048]{1,0:T(8,128)(2,1)} custom-call(s32[2]{0:T(128)S(1)} %pad_add_fusion.1.where, bf16[512,512]{1,0:T(8,128)(2,1)} %collective-permute-done.14.refs_0_, bf16[512,512]{1,0:T(8,128)(2,1)} %collective-permute-done.15.refs_1_, bf16[512,512]{1,0:T(8,128)(2,1)} %copy-done.11, bf16[512,512]{1,0:T(8,128)(2,1)S(1)} %collective-permute-done.10.refs_3_, ...), custom_call_target="tpu_custom_call" | custom-call | tf_op jit(solution)/shard_map/pallas_call | solution.py:41
  107.6 3.9 %shard_map.163 = (bf16[512,512]{1,0:T(8,128)(2,1)S(1)}, bf16[512,512]{1,0:T(8,128)(2,1)S(1)}) custom-call(s32[1]{0:T(128)} %constant.75.clone.1._, bf16[512,512]{1,0:T(8,128)(2,1)} %collective-permute-done.21.refs_0_, bf16[512,512]{1,0:T(8,128)(2,1)} %collective-permute-done.22.refs_1_, bf16[512,512]{1,0:T(8,128)(2,1)} %copy-done.11, ...), custom_call_target="tpu_custom_call" | custom-call | tf_op jit(solution)/shard_map/pallas_call | solution.py:41
  112.1 2.3 %fusion = (f32[64,2048]{1,0:T(8,128)}, f32[64,2048]{1,0:T(8,128)}, f32[64,2048]{1,0:T(8,128)}) fusion(f32[1,64,2048]{2,1,0:T(8,128)S(1)} %copy-done.10, f32[64,2048]{1,0:T(8,128)S(1)} %copy-done.13, f32[64,2048]{1,0:T(8,128)S(1)} %copy-done.14, bf16[64,2048]{1,0:T(8,128)(2,1)} %collective-permute-done.9, bf16[64,2048]{1,0:T(8,128)(2,1)S(1)} %add_convert_fusion, ...), kind=kLoop, calls=%fused_computation.2 | loop fusion | flops 1703936 | bytes 3670020 | tf_op jit(solution)/shard_map/add | solution.py:336
  114.7 2.0 %collective-permute-done.25.received = bf16[512,512]{1,0:T(8,128)(2,1)S(1)} collective-permute-done((bf16[512,512]{1,0:T(8,128)(2,1)}, bf16[512,512]{1,0:T(8,128)(2,1)S(1)}, u32[]{:S(2)}, u32[]{:S(2)}) %collective-permute-start.25) | collective-permute-done | bytes 524320 | tf_op jit(solution)/shard_map/ppermute | solution.py:20
  116.8 2.0 %shard_map.165 = (f32[512,256]{1,0:T(8,128)}, f32[512,256]{1,0:T(8,128)}, bf16[512,2048]{1,0:T(8,128)(2,1)}) custom-call(s32[2]{0:T(128)S(1)} %pad_add_fusion.where, f32[512,512]{1,0:T(8,128)S(1)} %shard_map.164.part, bf16[512,512]{1,0:T(8,128)(2,1)S(1)} %collective-permute-done.25.received, ...), custom_call_target="tpu_custom_call", output_to_operand_aliasing={{2}: (5, {})} | custom-call | tf_op jit(solution)/shard_map/pallas_call | solution.py:41
  (88 shorter events, 22.0 us)
Async XLA Ops:
  7.2 8.3 %collective-permute-start.4 = (bf16[9,512,512]{2,1,0:T(8,128)(2,1)}, bf16[9,512,512]{2,1,0:T(8,128)(2,1)}, u32[]{:S(2)}, u32[]{:S(2)}) collective-permute-start(bf16[9,512,512]{2,1,0:T(8,128)(2,1)} %get-tuple-element.77), channel_id=1, source_target_pairs={{0,4},{4,0},{1,5},{5,1},{2,6},{6,2},{3,7},{7,3},{8,12},{12,8},{9,1... | collective-permute-start | bytes 14155784 | tf_op jit(solution)/shard_map/ppermute | solution.py:20
  7.3 15.9 %collective-permute-start = (bf16[64,2048]{1,0:T(8,128)(2,1)S(1)}, bf16[64,2048]{1,0:T(8,128)(2,1)S(1)}, u32[]{:S(2)}, u32[]{:S(2)}) collective-permute-start(bf16[64,2048]{1,0:T(8,128)(2,1)S(1)} %bitcast_convert_fusion), channel_id=1, source_target_pairs={{0,64},{64,0},{128,192},{192,128},{1,65},{65,1},{129,193},{193,129... | collective-permute-start | bytes 786440 | tf_op jit(solution)/shard_map/ppermute | solution.py:291
  10.7 26.7 %collective-permute-start.1 = (bf16[512,512]{1,0:T(8,128)(2,1)S(1)}, bf16[512,512]{1,0:T(8,128)(2,1)S(1)}, u32[]{:S(2)}, u32[]{:S(2)}) collective-permute-start(bf16[512,512]{1,0:T(8,128)(2,1)S(1)} %shard_map.154.refs_0_), channel_id=1, source_target_pairs={{0,48},{16,0},{32,16},{48,32},{1,49},{17,1},{33,17},{49,33},{2,50}... | collective-permute-start | bytes 1572872 | tf_op jit(solution)/shard_map/ppermute | solution.py:20
  13.7 23.7 %collective-permute-start.2 = (bf16[512,512]{1,0:T(8,128)(2,1)S(1)}, bf16[512,512]{1,0:T(8,128)(2,1)S(1)}, u32[]{:S(2)}, u32[]{:S(2)}) collective-permute-start(bf16[512,512]{1,0:T(8,128)(2,1)S(1)} %shard_map.154.refs_0_), channel_id=1, source_target_pairs={{0,32},{16,48},{32,0},{48,16},{1,33},{17,49},{33,1},{49,17},{2,34}... | collective-permute-start | bytes 1572872 | tf_op jit(solution)/shard_map/ppermute | solution.py:20
  14.3 25.9 %collective-permute-start.3 = (bf16[512,512]{1,0:T(8,128)(2,1)S(1)}, bf16[512,512]{1,0:T(8,128)(2,1)S(1)}, u32[]{:S(2)}, u32[]{:S(2)}) collective-permute-start(bf16[512,512]{1,0:T(8,128)(2,1)S(1)} %shard_map.154.refs_0_), channel_id=1, source_target_pairs={{0,16},{16,32},{32,48},{48,0},{1,17},{17,33},{33,49},{49,1},{2,18}... | collective-permute-start | bytes 1572872 | tf_op jit(solution)/shard_map/ppermute | solution.py:20
  15.5 24.7 %collective-permute-start.5 = (bf16[512,512]{1,0:T(8,128)(2,1)}, bf16[512,512]{1,0:T(8,128)(2,1)S(1)}, u32[]{:S(2)}, u32[]{:S(2)}) collective-permute-start(bf16[512,512]{1,0:T(8,128)(2,1)} %get-tuple-element.95.grads.refs_0_), channel_id=1, source_target_pairs={{0,1},{1,2},{2,3},{3,0},{4,5},{5,6},{6,7},{7,4},{8,9},{9,10},{10,1... | collective-permute-start | bytes 1572872 | tf_op jit(solution)/shard_map/ppermute | solution.py:20
  23.3 21.2 %collective-permute-start.9 = (bf16[64,2048]{1,0:T(8,128)(2,1)S(1)}, bf16[64,2048]{1,0:T(8,128)(2,1)}, u32[]{:S(2)}, u32[]{:S(2)}) collective-permute-start(bf16[64,2048]{1,0:T(8,128)(2,1)S(1)} %add_convert_fusion), channel_id=1, source_target_pairs={{0,192},{64,128},{128,64},{192,0},{1,193},{65,129},{129,65},{193,1... | collective-permute-start | bytes 786440 | tf_op jit(solution)/shard_map/ppermute | solution.py:297
  40.5 13.9 %collective-permute-start.6 = (bf16[512,512]{1,0:T(8,128)(2,1)S(1)}, bf16[512,512]{1,0:T(8,128)(2,1)S(1)}, u32[]{:S(2)}, u32[]{:S(2)}) collective-permute-start(bf16[512,512]{1,0:T(8,128)(2,1)S(1)} %get-tuple-element.86), channel_id=1, source_target_pairs={{0,1},{1,2},{2,3},{3,0},{4,5},{5,6},{6,7},{7,4},{8,9},{9,10},{10,1... | collective-permute-start | bytes 1572872 | tf_op jit(solution)/shard_map/ppermute | solution.py:20
  41.1 14.8 %collective-permute-start.7 = (bf16[512,512]{1,0:T(8,128)(2,1)S(1)}, bf16[512,512]{1,0:T(8,128)(2,1)S(1)}, u32[]{:S(2)}, u32[]{:S(2)}) collective-permute-start(bf16[512,512]{1,0:T(8,128)(2,1)S(1)} %get-tuple-element.87), channel_id=1, source_target_pairs={{0,3},{1,0},{2,1},{3,2},{4,7},{5,4},{6,5},{7,6},{8,11},{9,8},{10,9... | collective-permute-start | bytes 1572872 | tf_op jit(solution)/shard_map/ppermute | solution.py:20
  42.6 13.5 %collective-permute-start.8 = (bf16[512,512]{1,0:T(8,128)(2,1)S(1)}, bf16[512,512]{1,0:T(8,128)(2,1)S(1)}, u32[]{:S(2)}, u32[]{:S(2)}) collective-permute-start(bf16[512,512]{1,0:T(8,128)(2,1)S(1)} %get-tuple-element.88.refs_4_), channel_id=1, source_target_pairs={{0,8},{8,0},{1,9},{9,1},{2,10},{10,2},{3,11},{11,3},{4,12},{12,4},... | collective-permute-start | bytes 1572872 | tf_op jit(solution)/shard_map/ppermute | solution.py:20
  44.5 25.6 %collective-permute-start.11 = (bf16[2,512,512]{2,1,0:T(8,128)(2,1)S(1)}, bf16[2,512,512]{2,1,0:T(8,128)(2,1)S(1)}, u32[]{:S(2)}, u32[]{:S(2)}) collective-permute-start(bf16[2,512,512]{2,1,0:T(8,128)(2,1)S(1)} %get-tuple-element.92), channel_id=1, source_target_pairs={{0,16},{16,32},{32,48},{48,0},{1,17},{17,33},{33,49},{49,1},{2,18}... | collective-permute-start | bytes 3145736 | tf_op jit(solution)/shard_map/ppermute | solution.py:20
  44.5 25.6 %collective-permute-start.12 = (bf16[2,512,512]{2,1,0:T(8,128)(2,1)S(1)}, bf16[2,512,512]{2,1,0:T(8,128)(2,1)S(1)}, u32[]{:S(2)}, u32[]{:S(2)}) collective-permute-start(bf16[2,512,512]{2,1,0:T(8,128)(2,1)S(1)} %get-tuple-element.93), channel_id=1, source_target_pairs={{0,48},{16,0},{32,16},{48,32},{1,49},{17,1},{33,17},{49,33},{2,50}... | collective-permute-start | bytes 3145736 | tf_op jit(solution)/shard_map/ppermute | solution.py:20
  56.1 14.1 %collective-permute-start.10 = (bf16[512,512]{1,0:T(8,128)(2,1)S(1)}, bf16[512,512]{1,0:T(8,128)(2,1)S(1)}, u32[]{:S(2)}, u32[]{:S(2)}) collective-permute-start(bf16[512,512]{1,0:T(8,128)(2,1)S(1)} %get-tuple-element.91), channel_id=1, source_target_pairs={{0,2},{1,3},{2,0},{3,1},{4,6},{5,7},{6,4},{7,5},{8,10},{9,11},{10,... | collective-permute-start | bytes 1572872 | tf_op jit(solution)/shard_map/ppermute | solution.py:20
  57.5 12.6 %collective-permute-start.13 = (bf16[512,512]{1,0:T(8,128)(2,1)S(1)}, bf16[512,512]{1,0:T(8,128)(2,1)S(1)}, u32[]{:S(2)}, u32[]{:S(2)}) collective-permute-start(bf16[512,512]{1,0:T(8,128)(2,1)S(1)} %collective-permute-done.6.refs_5_), channel_id=1, source_target_pairs={{0,8},{8,0},{1,9},{9,1},{2,10},{10,2},{3,11},{11,3},{4,12},{12,4},... | collective-permute-start | bytes 1572872 | tf_op jit(solution)/shard_map/ppermute | solution.py:20
  59.2 16.9 %collective-permute-start.20 = (bf16[512,512]{1,0:T(8,128)(2,1)S(1)}, bf16[512,512]{1,0:T(8,128)(2,1)S(1)}, u32[]{:S(2)}, u32[]{:S(2)}) collective-permute-start(bf16[512,512]{1,0:T(8,128)(2,1)S(1)} %collective-permute-done.5.refs_1_), channel_id=1, source_target_pairs={{0,4},{4,0},{1,5},{5,1},{2,6},{6,2},{3,7},{7,3},{8,12},{12,8},{9,1... | collective-permute-start | bytes 1572872 | tf_op jit(solution)/shard_map/ppermute | solution.py:20
  70.4 13.2 %collective-permute-start.18 = (bf16[512,512]{1,0:T(8,128)(2,1)S(1)}, bf16[512,512]{1,0:T(8,128)(2,1)S(1)}, u32[]{:S(2)}, u32[]{:S(2)}) collective-permute-start(bf16[512,512]{1,0:T(8,128)(2,1)S(1)} %get-tuple-element.102), channel_id=1, source_target_pairs={{0,16},{16,32},{32,48},{48,0},{1,17},{17,33},{33,49},{49,1},{2,18}... | collective-permute-start | bytes 1572872 | tf_op jit(solution)/shard_map/ppermute | solution.py:20
  70.5 24.7 %collective-permute-start.19 = (bf16[512,512]{1,0:T(8,128)(2,1)S(1)}, bf16[512,512]{1,0:T(8,128)(2,1)S(1)}, u32[]{:S(2)}, u32[]{:S(2)}) collective-permute-start(bf16[512,512]{1,0:T(8,128)(2,1)S(1)} %get-tuple-element.103), channel_id=1, source_target_pairs={{0,48},{16,0},{32,16},{48,32},{1,49},{17,1},{33,17},{49,33},{2,50}... | collective-permute-start | bytes 1572872 | tf_op jit(solution)/shard_map/ppermute | solution.py:20
  73.7 23.2 %collective-permute-start.16 = (bf16[512,512]{1,0:T(8,128)(2,1)S(1)}, bf16[512,512]{1,0:T(8,128)(2,1)S(1)}, u32[]{:S(2)}, u32[]{:S(2)}) collective-permute-start(bf16[512,512]{1,0:T(8,128)(2,1)S(1)} %collective-permute-done.7.refs_2_), channel_id=1, source_target_pairs={{0,8},{8,0},{1,9},{9,1},{2,10},{10,2},{3,11},{11,3},{4,12},{12,4},... | collective-permute-start | bytes 1572872 | tf_op jit(solution)/shard_map/ppermute | solution.py:20
  75.6 23.7 %collective-permute-start.14 = (bf16[512,512]{1,0:T(8,128)(2,1)}, bf16[512,512]{1,0:T(8,128)(2,1)}, u32[]{:S(2)}, u32[]{:S(2)}) collective-permute-start(bf16[512,512]{1,0:T(8,128)(2,1)} %get-tuple-element.95.grads.refs_0_), channel_id=1, source_target_pairs={{0,3},{1,0},{2,1},{3,2},{4,7},{5,4},{6,5},{7,6},{8,11},{9,8},{10,9... | collective-permute-start | bytes 1572872 | tf_op jit(solution)/shard_map/ppermute | solution.py:20
  76.1 23.2 %collective-permute-start.15 = (bf16[512,512]{1,0:T(8,128)(2,1)}, bf16[512,512]{1,0:T(8,128)(2,1)}, u32[]{:S(2)}, u32[]{:S(2)}) collective-permute-start(bf16[512,512]{1,0:T(8,128)(2,1)} %get-tuple-element.95.grads.refs_0_), channel_id=1, source_target_pairs={{0,2},{1,3},{2,0},{3,1},{4,6},{5,7},{6,4},{7,5},{8,10},{9,11},{10,... | collective-permute-start | bytes 1572872 | tf_op jit(solution)/shard_map/ppermute | solution.py:20
  83.6 15.7 %collective-permute-start.17 = (bf16[512,512]{1,0:T(8,128)(2,1)S(1)}, bf16[512,512]{1,0:T(8,128)(2,1)S(1)}, u32[]{:S(2)}, u32[]{:S(2)}) collective-permute-start(bf16[512,512]{1,0:T(8,128)(2,1)S(1)} %collective-permute-done.10.refs_3_), channel_id=1, source_target_pairs={{0,8},{8,0},{1,9},{9,1},{2,10},{10,2},{3,11},{11,3},{4,12},{12,4},... | collective-permute-start | bytes 1572872 | tf_op jit(solution)/shard_map/ppermute | solution.py:20
  99.3 8.3 %collective-permute-start.21 = (bf16[512,512]{1,0:T(8,128)(2,1)}, bf16[512,512]{1,0:T(8,128)(2,1)}, u32[]{:S(2)}, u32[]{:S(2)}) collective-permute-start(bf16[512,512]{1,0:T(8,128)(2,1)} %collective-permute-done.14.refs_0_), channel_id=1, source_target_pairs={{0,4},{4,0},{1,5},{5,1},{2,6},{6,2},{3,7},{7,3},{8,12},{12,8},{9,1... | collective-permute-start | bytes 1572872 | tf_op jit(solution)/shard_map/ppermute | solution.py:20
  99.4 8.2 %collective-permute-start.22 = (bf16[512,512]{1,0:T(8,128)(2,1)}, bf16[512,512]{1,0:T(8,128)(2,1)}, u32[]{:S(2)}, u32[]{:S(2)}) collective-permute-start(bf16[512,512]{1,0:T(8,128)(2,1)} %collective-permute-done.15.refs_1_), channel_id=1, source_target_pairs={{0,4},{4,0},{1,5},{5,1},{2,6},{6,2},{3,7},{7,3},{8,12},{12,8},{9,1... | collective-permute-start | bytes 1572872 | tf_op jit(solution)/shard_map/ppermute | solution.py:20
  102.6 14.2 %collective-permute-start.25 = (bf16[512,512]{1,0:T(8,128)(2,1)}, bf16[512,512]{1,0:T(8,128)(2,1)S(1)}, u32[]{:S(2)}, u32[]{:S(2)}) collective-permute-start(bf16[512,512]{1,0:T(8,128)(2,1)} %copy-done.6), channel_id=1, source_target_pairs={{0,8},{8,0},{1,9},{9,1},{2,10},{10,2},{3,11},{11,3},{4,12},{12,4},... | collective-permute-start | bytes 1572872 | tf_op jit(solution)/shard_map/ppermute | solution.py:20
  (22 other events, 284.7 us)
